TPU v7x, 32 devices: a whole 2x2x4 slice. The times are simulated.
32 devices in a mesh: freq: 4 (over z), rcv: 8 (over y, x, core).
Axes of the slice: x: 2, y: 2, z: 4, core: 2. Of those that a mesh axis runs over, the one named last changes fastest.
Arguments:
- spectra: float32 [64, 2, 512, 512], P('freq', None, 'rcv'), may hold values from -0.5 to 0.5
- counts: int32 [4], replicated, may hold values from 1 to 16, 32 in all
- partner: int32 [512], replicated, may hold values from 0 to 511, as said below
- recorded: float32 [512, 512, 512], P('freq', 'rcv'), may hold values from -3 to 3
- gain_index: int32 [512, 512], P('freq', 'rcv'), may hold values from 0 to 15
- gain_table: float32 [2, 16], replicated, may hold values from 0.5 to 1.5
Outputs:
- primaries: float32 [512, 512, 512], P('freq', 'rcv')
Inputs may be any that keep to these rules, and one draw needn't show every extreme that they name: `counts`: the bands hold 32 frequencies together, and some band holds exactly 16. `partner`: A permutation that maps each aligned block of 64 indices onto itself.
All inputs are finite; a program needn't handle non-finite values.
Results may differ from a plain program's by a relative error of at most 0.00005.
Values sent between devices are 32-bit elements; how exact they have to be, the bound alone decides.
No kernel may reach another device: no remote copies, remote signals or barrier semaphores. Data moves between devices by JAX's collectives and lax.ppermute only.
A program may use at most 128 MiB of HBM per device.

v0:
```python
import functools

import jax
import jax.numpy as jnp
from jax import lax
from jax.experimental import pallas as pl
from jax.experimental.pallas import tpu as pltpu
from jax.sharding import PartitionSpec as P

LEVELS = 16
PICK = 256
LANES = 128
VMEM_BYTES = 56 * 1024 * 1024


def time_table(bin_numbers, samples):
    phases = bin_numbers[:, None] * jnp.arange(samples, dtype=jnp.int32)[None, :] % samples
    angles = 2.0 * jnp.pi / samples * phases.astype(jnp.float32)
    return jnp.stack([jnp.cos(angles), -jnp.sin(angles)], axis=1)


def split(values):
    high = values.astype(jnp.bfloat16)
    return high, (values - high.astype(jnp.float32)).astype(jnp.bfloat16)


def mm(left, right):
    return jnp.dot(left, right, preferred_element_type=jnp.float32)


def gather_table(partner_column, start, size):
    columns = lax.broadcasted_iota(jnp.int32, (size, size), 1) + start
    return jnp.where(partner_column == columns, 1.0, 0.0).astype(jnp.bfloat16)


def scatter_table(partner_row, start, size):
    rows = lax.broadcasted_iota(jnp.int32, (size, size), 0) + start
    return jnp.where(partner_row == rows, 1.0, 0.0).astype(jnp.bfloat16)


def gains_kernel(table_ref, index_ref, column_ref, out_ref, whole_ref, *, source_tiles):
    side = whole_ref.shape[0]
    receiver_tile, source_tile = index_ref.shape[1:]
    receiver_tiles = side // receiver_tile
    for a in range(source_tiles):
        for i in range(receiver_tiles):
            whole_ref[i * receiver_tile : (i + 1) * receiver_tile, a * source_tile : (a + 1) * source_tile] = (
                index_ref[a * receiver_tiles + i].astype(jnp.float32)
            )
    pick = min(PICK, side)
    for start in range(0, side, pick):
        rows = slice(start, start + pick)
        table = gather_table(column_ref[rows, :], start, pick)
        levels = mm(table, whole_ref[rows, :].astype(jnp.bfloat16))
        first = jnp.zeros_like(levels)
        second = jnp.zeros_like(levels)
        for level in range(LEVELS):
            here = levels == float(level)
            first = jnp.where(here, 0.5 * table_ref[0, level], first)
            second = jnp.where(here, 0.5 * table_ref[1, level], second)
        out_ref[0, rows, :] = first
        out_ref[1, rows, :] = second


def multiples_kernel(live_ref, data_ref, column_ref, row_ref, gains_ref, out_ref, wh, wl, uh, ul, y1, y2, *, source_tiles):
    receiver_tiles, _, receiver_tile, side = data_ref.shape
    source_tile = side // source_tiles
    pick = min(PICK, side)

    @pl.when(live_ref[0] == 0)
    def _():
        out_ref[...] = jnp.zeros_like(out_ref)

    @pl.when(live_ref[0] != 0)
    def _():
        for i in range(receiver_tiles):
            top = slice(i * receiver_tile, (i + 1) * receiver_tile)
            low = slice(side + i * receiver_tile, side + (i + 1) * receiver_tile)
            real_high, real_low = split(data_ref[i, 0])
            imag_high, imag_low = split(data_ref[i, 1])
            wh[top, :side] = real_high
            wh[low, side:] = real_high
            wh[top, side:] = imag_high
            wh[low, :side] = -imag_high
            wl[top, :side] = real_low
            wl[low, side:] = real_low
            wl[top, side:] = imag_low
            wl[low, :side] = -imag_low
        for start in range(0, side, pick):
            rows = slice(start, start + pick)
            table = gather_table(column_ref[rows, :], start, pick)
            uh[rows, :] = mm(table, wh[rows, :]).astype(jnp.bfloat16)
            ul[rows, :] = mm(table, wl[rows, :]).astype(jnp.bfloat16)

        def product(result):
            for start in range(0, 2 * side, PICK):
                cols = slice(start, start + PICK)
                result[:, cols] = mm(uh[...], wh[:, cols]) + mm(uh[...], wl[:, cols]) + mm(ul[...], wh[:, cols])

        product(y1)
        for start in range(0, side, 64):
            rows = slice(start, start + 64)
            uh[rows, :], ul[rows, :] = split(y1[rows, :])
        product(y2)
        block = 128
        for q in range(0, side, block):
            for s in range(0, side, block):
                qs, ss = slice(q, q + block), slice(s, s + block)
                first_gain, second_gain = gains_ref[0, qs, ss], gains_ref[1, qs, ss]
                for c in range(2):
                    qc, sc = slice(c * side + q, c * side + q + block), slice(c * side + s, c * side + s + block)
                    value = first_gain * (y1[qs, sc] + y1[ss, qc].T) + second_gain * (y2[qs, sc] + y2[ss, qc].T)
                    uh[qs, sc], ul[qs, sc] = split(value)
        for start in range(0, side, pick):
            rows = slice(start, start + pick)
            table = scatter_table(row_ref[:, rows], start, pick)
            for c in range(2):
                cols = slice(c * side, (c + 1) * side)
                natural = mm(table, uh[rows, cols]) + mm(table, ul[rows, cols])
                for i in range(pick // receiver_tile):
                    tile = start // receiver_tile + i
                    for a in range(source_tiles):
                        out_ref[a * receiver_tiles + tile, c] = natural[
                            i * receiver_tile : (i + 1) * receiver_tile, a * source_tile : (a + 1) * source_tile
                        ]


def synthesis_kernel(*refs, parts, receiver_tile):
    coefs = refs[:parts]
    table_ref, recorded_ref, out_ref, lines, table_high, table_low = refs[parts:]
    depth = table_ref.shape[0]
    part_depth = depth // parts
    source_tile = coefs[0].shape[1]

    @pl.when(pl.program_id(0) == 0)
    def _():
        for r in range(receiver_tile):
            columns = [ref[pl.ds(r, part_depth, stride=receiver_tile), :] for ref in coefs]
            column = columns[0] if parts == 1 else jnp.concatenate(columns, axis=0)
            for g in range(lines.shape[0]):
                lines[g, pl.ds(r, source_tile, stride=receiver_tile), :] = column[g * LANES : (g + 1) * LANES].T
        high, low = split(table_ref[...])
        table_high[:depth, :] = high
        table_high[depth:, :] = high
        table_low[...] = low

    size = recorded_ref.shape[0] * receiver_tile
    rows = pl.ds(pl.multiple_of(pl.program_id(0) * size, size), size)
    high, low = split(jnp.concatenate([lines[g, rows, :] for g in range(lines.shape[0])], axis=1))
    both = jnp.concatenate([high, low], axis=1)
    total = mm(both, table_high[...]) + mm(high, table_low[...])
    out_ref[...] = recorded_ref[...] - total.reshape(recorded_ref.shape)


def params():
    return pltpu.CompilerParams(vmem_limit_bytes=VMEM_BYTES)


def whole_in(space=pltpu.VMEM):
    return pl.BlockSpec(memory_space=space)


def on_device(spectra, counts, partner, recorded, gain_index, gain_table):
    freq_count = lax.axis_size("freq")
    rcv_count = lax.axis_size("rcv")
    freq_rank = lax.axis_index("freq")
    rcv_rank = lax.axis_index("rcv")
    capacity, _, receiver_tile, side = spectra.shape
    source_tile, _, samples = recorded.shape
    parts = capacity // rcv_count
    senders = freq_count * rcv_count
    offsets = jnp.cumsum(counts) - counts
    own_count = counts[freq_rank]
    column = partner[:, None]
    row = partner[None, :]

    gathered = [
        lax.all_to_all(
            spectra[part * rcv_count : (part + 1) * rcv_count], "rcv", split_axis=0, concat_axis=0, tiled=True
        )
        for part in range(parts)
    ]
    tiles = lax.all_gather(gain_index.T, ("freq", "rcv"), axis=0, tiled=False)
    gains = pl.pallas_call(
        functools.partial(gains_kernel, source_tiles=freq_count),
        out_shape=jax.ShapeDtypeStruct((2, side, side), jnp.float32),
        in_specs=[whole_in(pltpu.SMEM), whole_in(), whole_in()],
        out_specs=whole_in(),
        scratch_shapes=[pltpu.VMEM((side, side), jnp.float32)],
        compiler_params=params(),
        name="gains",
    )(gain_table, tiles, column)

    multiples = pl.pallas_call(
        functools.partial(multiples_kernel, source_tiles=freq_count),
        out_shape=jax.ShapeDtypeStruct((senders, 2, receiver_tile, source_tile), jnp.float32),
        in_specs=[whole_in(pltpu.SMEM), whole_in(), whole_in(), whole_in(), whole_in()],
        out_specs=whole_in(),
        scratch_shapes=[
            pltpu.VMEM((2 * side, 2 * side), jnp.bfloat16),
            pltpu.VMEM((2 * side, 2 * side), jnp.bfloat16),
            pltpu.VMEM((side, 2 * side), jnp.bfloat16),
            pltpu.VMEM((side, 2 * side), jnp.bfloat16),
            pltpu.VMEM((side, 2 * side), jnp.float32),
            pltpu.VMEM((side, 2 * side), jnp.float32),
        ],
        compiler_params=params(),
        name="multiples",
    )
    received = []
    bins = []
    sender = jnp.arange(senders, dtype=jnp.int32)
    for part in range(parts):
        live = (part * rcv_count + rcv_rank < own_count).astype(jnp.int32).reshape(1)
        sent = multiples(live, gathered[part], column, row, gains)
        arrived = lax.all_to_all(sent, ("freq", "rcv"), split_axis=0, concat_axis=0, tiled=True)
        received.append(arrived.reshape(senders * 2 * receiver_tile, source_tile))
        bins.append(offsets[sender // rcv_count] + part * rcv_count + sender % rcv_count + 1)

    table = time_table(jnp.concatenate(bins), samples).reshape(-1, samples)
    depth = table.shape[0]
    step = 8
    block = pl.BlockSpec((step, receiver_tile, samples), lambda n: (n, 0, 0))
    return pl.pallas_call(
        functools.partial(synthesis_kernel, parts=parts, receiver_tile=receiver_tile),
        out_shape=jax.ShapeDtypeStruct(recorded.shape, jnp.float32),
        grid=(source_tile // step,),
        in_specs=[whole_in()] * parts + [whole_in(), block],
        out_specs=block,
        scratch_shapes=[
            pltpu.VMEM((depth // LANES, source_tile * receiver_tile, LANES), jnp.float32),
            pltpu.VMEM((2 * depth, samples), jnp.bfloat16),
            pltpu.VMEM((depth, samples), jnp.bfloat16),
        ],
        compiler_params=params(),
        name="synthesis",
    )(*received, table, recorded)


def solution(mesh):
    placed = (P("freq", None, "rcv", None), P(), P(), P("freq", "rcv", None), P("freq", "rcv"), P())
    return jax.shard_map(
        on_device, mesh=mesh, in_specs=placed, out_specs=P("freq", "rcv", None), check_vma=False
    )
```

profile of v0, /device:TPU:0, one launch (start us, length us, event | category | flops | bytes accessed | tf_op | source)
XLA Modules:
  0.0 241.6 jit_solution(15921076274754340463)
XLA Ops:
  6.5 5.0 %fusion.9 = (f32[8,2,64,512]{3,2,1,0:T(8,128)}, f32[8,2,64,512]{3,2,1,0:T(8,128)}) fusion(f32[16,2,64,512]{3,2,1,0:T(8,128)} %param.6), kind=kLoop, calls=%fused_computation.26 | loop fusion | bytes 8388608 | tf_op jit(solution)/shard_map/slice | solution.py:179
  11.5 5.2 %all-to-all-start.2 = ((f32[8,2,64,512]{3,2,1,0:T(8,128)}), f32[8,2,64,512]{3,2,1,0:T(8,128)S(1)}, u32[]{:S(2)}, u32[]{:S(2)}) async-start(f32[8,2,64,512]{3,2,1,0:T(8,128)} %get-tuple-element.7), calls=%async_computation.2 | async-start | bytes 4194304 | tf_op jit(solution)/shard_map/all_to_all | solution.py:178
  16.7 0.7 all-gather.3.cloned.1.call-update
  17.4 26.2 %all-to-all-done.2.data_ref = f32[8,2,64,512]{3,2,1,0:T(8,128)S(1)} async-done(((f32[8,2,64,512]{3,2,1,0:T(8,128)}), f32[8,2,64,512]{3,2,1,0:T(8,128)S(1)}, u32[]{:S(2)}, u32[]{:S(2)}) %all-to-all-start.2) | async-done | bytes 2097184 | tf_op jit(solution)/shard_map/all_to_all | solution.py:178
  43.6 1.3 copy-done.1
  44.9 4.4 %all-to-all-start = ((f32[8,2,64,512]{3,2,1,0:T(8,128)}), f32[8,2,64,512]{3,2,1,0:T(8,128)}, u32[]{:S(2)}, u32[]{:S(2)}) async-start(f32[8,2,64,512]{3,2,1,0:T(8,128)} %get-tuple-element.8), calls=%async_computation | async-start | bytes 4194304 | tf_op jit(solution)/shard_map/all_to_all | solution.py:178
  49.3 0.6 dynamic_slice.3
  50.6 0.9 copy.11.column_ref
  51.4 35.2 %all-gather.3.cloned.1.call-done = s32[2048,128]{1,0:T(8,128)} async-done(((s32[64,128]{1,0:T(8,128)}), s32[2048,128]{1,0:T(8,128)}) %all-gather.3.cloned.1.call-update) | async-done | bytes 1048592 | tf_op jit(solution)/shard_map/all_gather | solution.py:183
  86.7 4.4 %gains.1.gains_ref = f32[2,512,512]{2,1,0:T(8,128)} custom-call(f32[2,16]{1,0:T(2,128)} %table_ref.1, s32[32,64,128]{2,1,0:T(8,128)} %bitcast.20, s32[512,1]{1,0:T(8,128)} %copy.11.column_ref), custom_call_target="tpu_custom_call" | custom-call | tf_op jit(solution)/shard_map/gains/pallas_call | solution.py:184
  91.1 12.1 %multiples.3 = f32[32,2,64,128]{3,2,1,0:T(8,128)} custom-call(s32[1]{0:T(128)} %bitcast.7.live_ref, f32[8,2,64,512]{3,2,1,0:T(8,128)} %copy-done.1, s32[512,1]{1,0:T(8,128)} %copy.11.column_ref, s32[1,512]{1,0:T(1,128)} %bitcast.22, f32[2,512,512]{2,1,0:T(8,128)} %gains.1.gains_ref), custom_call_target="tpu_custom_call" | custom-call | tf_op jit(solution)/shard_map/multiples/pallas_call | solution.py:215
  103.2 2.7 %all-to-all-start.3 = ((f32[32,2,64,128]{3,2,1,0:T(8,128)}), f32[32,2,64,128]{3,2,1,0:T(8,128)S(1)}, u32[]{:S(2)}, u32[]{:S(2)}) async-start(f32[32,2,64,128]{3,2,1,0:T(8,128)} %multiples.3), calls=%async_computation.3 | async-start | bytes 4194304 | tf_op jit(solution)/shard_map/all_to_all | solution.py:216
  106.5 12.0 %multiples.2 = f32[32,2,64,128]{3,2,1,0:T(8,128)} custom-call(s32[1]{0:T(128)} %bitcast.1.live_ref, f32[8,2,64,512]{3,2,1,0:T(8,128)} %all-to-all-done.data_ref, s32[512,1]{1,0:T(8,128)} %copy.11.column_ref, s32[1,512]{1,0:T(1,128)} %bitcast.23, f32[2,512,512]{2,1,0:T(8,128)} %gains.1.gains_ref), custom_call_target="tpu_custom_call" | custom-call | tf_op jit(solution)/shard_map/multiples/pallas_call | solution.py:215
  118.6 36.3 %all-to-all-done.3 = f32[32,2,64,128]{3,2,1,0:T(8,128)S(1)} async-done(((f32[32,2,64,128]{3,2,1,0:T(8,128)}), f32[32,2,64,128]{3,2,1,0:T(8,128)S(1)}, u32[]{:S(2)}, u32[]{:S(2)}) %all-to-all-start.3) | async-done | bytes 2097184 | tf_op jit(solution)/shard_map/all_to_all | solution.py:216
  154.8 1.4 copy-done
  156.2 4.0 %all-to-all-start.1 = ((f32[32,2,64,128]{3,2,1,0:T(8,128)}), f32[32,2,64,128]{3,2,1,0:T(8,128)}, u32[]{:S(2)}, u32[]{:S(2)}) async-start(f32[32,2,64,128]{3,2,1,0:T(8,128)} %multiples.2), calls=%async_computation.1 | async-start | bytes 4194304 | tf_op jit(solution)/shard_map/all_to_all | solution.py:216
  160.2 0.2 reduce-window.9
  160.4 0.6 fusion.10
  161.0 2.5 %add_add_fusion.1 = (s32[32]{0:T(128)S(1)}, s32[32]{0:T(128)S(1)}) fusion(s32[]{:T(128)} %bitcast.14, s32[]{:T(128)} %bitcast.13, s32[]{:T(128)} %bitcast.12, s32[]{:T(128)} %bitcast.11), kind=kLoop, calls=%fused_computation.25 | loop fusion | flops 800 | bytes 272 | tf_op jit(solution)/shard_map/add | solution.py:218
  163.6 0.6 fusion.6
  164.2 0.2 copy.13
  164.5 0.9 reshape.190.refs_2_
  165.3 43.7 %all-to-all-done.1 = f32[32,2,64,128]{3,2,1,0:T(8,128)} async-done(((f32[32,2,64,128]{3,2,1,0:T(8,128)}), f32[32,2,64,128]{3,2,1,0:T(8,128)}, u32[]{:S(2)}, u32[]{:S(2)}) %all-to-all-start.1) | async-done | bytes 2097184 | tf_op jit(solution)/shard_map/all_to_all | solution.py:216
  209.1 25.7 %synthesis.1 = f32[128,64,512]{2,1,0:T(8,128)} custom-call(f32[4096,128]{1,0:T(8,128)} %bitcast.6.refs_0_, f32[4096,128]{1,0:T(8,128)} %bitcast.19, f32[128,512]{1,0:T(8,128)} %reshape.190.refs_2_, f32[128,64,512]{2,1,0:T(8,128)} %refs_3_.1), custom_call_target="tpu_custom_call" | custom-call | tf_op jit(solution)/shard_map/synthesis/pallas_call | solution.py:224
  (12 shorter events, 0.2 us)
Async XLA Ops:
  11.5 32.1 %all-to-all-start.2 = ((f32[8,2,64,512]{3,2,1,0:T(8,128)}), f32[8,2,64,512]{3,2,1,0:T(8,128)S(1)}, u32[]{:S(2)}, u32[]{:S(2)}) async-start(f32[8,2,64,512]{3,2,1,0:T(8,128)} %get-tuple-element.7), calls=%async_computation.2 | async-start | bytes 4194304 | tf_op jit(solution)/shard_map/all_to_all | solution.py:178
  16.7 70.0 %all-gather.3.cloned.1.call-start = ((), (), s32[]{:S(2)}) async-start(), calls=%async_computation.4 | async-start | bytes 1081344 | tf_op jit(solution)/shard_map/all_gather | solution.py:183
  43.5 1.4 copy-start.1
  43.6 5.7 %copy-start.3 = (s32[4]{0:T(128)S(1)}, s32[4]{0:T(128)}, u32[]{:S(2)}) copy-start(s32[4]{0:T(128)} %param.7) | copy-start | bytes 52
  43.6 7.0 %copy-start.2 = (s32[512]{0:T(512)S(1)}, s32[512]{0:T(512)}, u32[]{:S(2)}) copy-start(s32[512]{0:T(512)} %param.8) | copy-start | bytes 6148
  44.9 58.3 %all-to-all-start = ((f32[8,2,64,512]{3,2,1,0:T(8,128)}), f32[8,2,64,512]{3,2,1,0:T(8,128)}, u32[]{:S(2)}, u32[]{:S(2)}) async-start(f32[8,2,64,512]{3,2,1,0:T(8,128)} %get-tuple-element.8), calls=%async_computation | async-start | bytes 4194304 | tf_op jit(solution)/shard_map/all_to_all | solution.py:178
  103.2 51.7 %all-to-all-start.3 = ((f32[32,2,64,128]{3,2,1,0:T(8,128)}), f32[32,2,64,128]{3,2,1,0:T(8,128)S(1)}, u32[]{:S(2)}, u32[]{:S(2)}) async-start(f32[32,2,64,128]{3,2,1,0:T(8,128)} %multiples.3), calls=%async_computation.3 | async-start | bytes 4194304 | tf_op jit(solution)/shard_map/all_to_all | solution.py:216
  154.8 1.4 copy-start
  156.2 52.9 %all-to-all-start.1 = ((f32[32,2,64,128]{3,2,1,0:T(8,128)}), f32[32,2,64,128]{3,2,1,0:T(8,128)}, u32[]{:S(2)}, u32[]{:S(2)}) async-start(f32[32,2,64,128]{3,2,1,0:T(8,128)} %multiples.2), calls=%async_computation.1 | async-start | bytes 4194304 | tf_op jit(solution)/shard_map/all_to_all | solution.py:216
Sparse Core Ops, SparseCore 0:
  20.4 66.2 all-gather.2
where the time goes:
time: 242 us
  waiting for transfers between devices  142 us (59%)
  Pallas kernels  54.3 us (22%)
  starting transfers between devices  16.3 us (7%)
  between operations  14.7 us (6%)
  local copies, waits for them, and re-layouts  10.9 us (5%)
  other arithmetic  3.37 us (1%)
    all_to_all x2, waiting for transfers between devices, on_device(): lax.all_to_all(sent, ('freq', 'rcv'), split_axis=0, concat_axis=0, tiled=...  80 us
    all_gather x1, waiting for transfers between devices, on_device(): tiles = lax.all_gather(gain_index.T, ('freq', 'rcv'), axis=0, tiled=False)  35.2 us
    all_to_all x2, waiting for transfers between devices, on_device(): lax.all_to_all(spectra[part * rcv_count:(part + 1) * rcv_count], 'rcv', s...  26.2 us
    pallas_call x1, Pallas kernels, on_device(): pl.pallas_call(functools.partial(synthesis_kernel, parts=parts, receiver_...  25.7 us
    pallas_call x2, Pallas kernels, on_device(): sent = multiples(live, gathered[part], column, row, gains)  24.1 us
    all_to_all x2, starting transfers between devices, on_device(): lax.all_to_all(spectra[part * rcv_count:(part + 1) * rcv_count], 'rcv', s...  9.53 us
    all_to_all x2, starting transfers between devices, on_device(): lax.all_to_all(sent, ('freq', 'rcv'), split_axis=0, concat_axis=0, tiled=...  6.73 us
    slice x1, local copies, waits for them, and re-layouts, on_device(): spectra[part * rcv_count:(part + 1) * rcv_count]  4.95 us
  transfers between devices with their start and end apart: 5, of which 4 were waited for; matrix products, arithmetic and copies ran while one was open for 3% of the time, Pallas kernels for 12%

commit v1 on v0

v1 whole, which is shorter than its diff:
```python
import functools

import jax
import jax.numpy as jnp
from jax import lax
from jax.experimental import pallas as pl
from jax.experimental.pallas import tpu as pltpu
from jax.sharding import PartitionSpec as P

LEVELS = 16
PICK = 256
LANES = 128


def time_table(bin_numbers, samples):
    phases = bin_numbers[:, None] * jnp.arange(samples, dtype=jnp.int32)[None, :] % samples
    angles = 2.0 * jnp.pi / samples * phases.astype(jnp.float32)
    return jnp.stack([jnp.cos(angles), -jnp.sin(angles)], axis=1)


def split(values):
    high = values.astype(jnp.bfloat16)
    return high, (values - high.astype(jnp.float32)).astype(jnp.bfloat16)


def mm(left, right):
    return jnp.dot(left, right, preferred_element_type=jnp.float32)


def gather_table(partner_column, start, size):
    columns = lax.broadcasted_iota(jnp.int32, (size, size), 1) + start
    return jnp.where(partner_column == columns, 1.0, 0.0).astype(jnp.bfloat16)


def scatter_table(partner_row, start, size):
    rows = lax.broadcasted_iota(jnp.int32, (size, size), 0) + start
    return jnp.where(partner_row == rows, 1.0, 0.0).astype(jnp.bfloat16)


def gains_kernel(place_ref, table_ref, near_ref, far_ref, column_ref, out_ref, tiles_ref, *, source_tiles):
    receiver_tile, source_tile = near_ref.shape[2:]
    side = source_tiles * source_tile
    receiver_tiles = side // receiver_tile
    for half, ref in enumerate((near_ref, far_ref)):
        for h in range(ref.shape[0]):
            for e in range(source_tiles):
                tile = (place_ref[0] ^ e) * receiver_tiles + (place_ref[1] ^ (2 * h + half))
                tiles_ref[tile] = ref[h, e].astype(jnp.float32)
    pick = min(PICK, side)
    for start in range(0, side, pick):
        rows = slice(start, start + pick)
        table = gather_table(column_ref[rows, :], start, pick)
        first_tile = start // receiver_tile
        for a in range(source_tiles):
            cols = slice(a * source_tile, (a + 1) * source_tile)
            lo = a * receiver_tiles + first_tile
            natural = tiles_ref[lo : lo + pick // receiver_tile].reshape(pick, source_tile)
            levels = mm(table, natural.astype(jnp.bfloat16))
            first = jnp.zeros_like(levels)
            second = jnp.zeros_like(levels)
            for level in range(LEVELS):
                here = levels == float(level)
                first = jnp.where(here, 0.5 * table_ref[0, level], first)
                second = jnp.where(here, 0.5 * table_ref[1, level], second)
            out_ref[0, rows, cols] = first
            out_ref[1, rows, cols] = second


def multiples_kernel(live_ref, order_ref, column_ref, row_ref, gains_ref, *refs, source_tiles):
    data, (out_ref, wh, wl, uh, ul, y1, y2) = refs[:-7], refs[-7:]
    receiver_tiles = len(data)
    _, receiver_tile, side = data[0].shape
    source_tile = side // source_tiles
    pick = min(PICK, side)

    @pl.when(live_ref[0] == 0)
    def _():
        out_ref[...] = jnp.zeros_like(out_ref)

    @pl.when(live_ref[0] != 0)
    def _():
        for i in range(receiver_tiles):
            first_row = pl.multiple_of(order_ref[i] * receiver_tile, receiver_tile)
            top = pl.ds(first_row, receiver_tile)
            low = pl.ds(side + first_row, receiver_tile)
            real_high, real_low = split(data[i][0])
            imag_high, imag_low = split(data[i][1])
            wh[top, :side] = real_high
            wh[low, side:] = real_high
            wh[top, side:] = imag_high
            wh[low, :side] = -imag_high
            wl[top, :side] = real_low
            wl[low, side:] = real_low
            wl[top, side:] = imag_low
            wl[low, :side] = -imag_low
        for start in range(0, side, pick):
            rows = slice(start, start + pick)
            table = gather_table(column_ref[rows, :], start, pick)
            uh[rows, :] = mm(table, wh[rows, :]).astype(jnp.bfloat16)
            ul[rows, :] = mm(table, wl[rows, :]).astype(jnp.bfloat16)

        def product(result):
            for start in range(0, 2 * side, PICK):
                cols = slice(start, start + PICK)
                result[:, cols] = mm(uh[...], wh[:, cols]) + mm(uh[...], wl[:, cols]) + mm(ul[...], wh[:, cols])

        product(y1)
        for start in range(0, side, 64):
            rows = slice(start, start + 64)
            uh[rows, :], ul[rows, :] = split(y1[rows, :])
        product(y2)
        block = 128
        for q in range(0, side, block):
            for s in range(0, side, block):
                qs, ss = slice(q, q + block), slice(s, s + block)
                first_gain, second_gain = gains_ref[0, qs, ss], gains_ref[1, qs, ss]
                for c in range(2):
                    qc, sc = slice(c * side + q, c * side + q + block), slice(c * side + s, c * side + s + block)
                    value = first_gain * (y1[qs, sc] + y1[ss, qc].T) + second_gain * (y2[qs, sc] + y2[ss, qc].T)
                    uh[qs, sc], ul[qs, sc] = split(value)
        for start in range(0, side, pick):
            rows = slice(start, start + pick)
            table = scatter_table(row_ref[:, rows], start, pick)
            for c in range(2):
                cols = slice(c * side, (c + 1) * side)
                natural = mm(table, uh[rows, cols]) + mm(table, ul[rows, cols])
                for i in range(pick // receiver_tile):
                    tile = start // receiver_tile + i
                    for a in range(source_tiles):
                        out_ref[a * receiver_tiles + tile, c] = natural[
                            i * receiver_tile : (i + 1) * receiver_tile, a * source_tile : (a + 1) * source_tile
                        ]


def synthesis_kernel(coef_ref, table_ref, base_ref, out_ref, lines, tables, *, receiver_tile, step):
    depth = table_ref.shape[0]
    source_tile = coef_ref.shape[1]

    @pl.when(pl.program_id(0) == 0)
    def _():
        for r in range(receiver_tile):
            column = coef_ref[pl.ds(r, depth, stride=receiver_tile), :]
            high = column.astype(jnp.bfloat16).astype(jnp.float32)
            both = jnp.concatenate([high, column - high], axis=0)
            for g in range(lines.shape[0]):
                lines[g, pl.ds(r, source_tile, stride=receiver_tile), :] = both[g * LANES : (g + 1) * LANES].T
        high, low = split(table_ref[...])
        tables[:depth, :] = high
        tables[depth : 2 * depth, :] = high
        tables[2 * depth :, :] = low

    size = step * receiver_tile
    rows = pl.ds(pl.multiple_of(pl.program_id(0) * size, size), size)
    both = jnp.concatenate([lines[g, rows, :] for g in range(lines.shape[0])], axis=1).astype(jnp.bfloat16)
    total = mm(jnp.concatenate([both, both[:, :depth]], axis=1), tables[...])

    def mine(ref):
        whole = ref.shape[0] != step
        return pl.ds(pl.multiple_of(pl.program_id(0) * step, step), step) if whole else slice(None)

    out_ref[mine(out_ref)] = base_ref[mine(base_ref)] - total.reshape(step, receiver_tile, -1)


def params(mebibytes):
    return pltpu.CompilerParams(vmem_limit_bytes=mebibytes * 1024 * 1024)


def whole_in(space=pltpu.VMEM):
    return pl.BlockSpec(memory_space=space)


def exchange(array, axis, distance):
    return lax.ppermute(array, axis, [(i, i ^ distance) for i in range(lax.axis_size(axis))])


def on_device(spectra, counts, partner, recorded, gain_index, gain_table):
    freq_count = lax.axis_size("freq")
    rcv_count = lax.axis_size("rcv")
    freq_rank = lax.axis_index("freq")
    rcv_rank = lax.axis_index("rcv")
    capacity, _, receiver_tile, side = spectra.shape
    source_tile, _, samples = recorded.shape
    parts = capacity // rcv_count
    senders = freq_count * rcv_count
    offsets = jnp.cumsum(counts) - counts
    own_count = counts[freq_rank]
    column = partner[:, None]
    row = partner[None, :]
    place = jnp.stack([freq_rank, rcv_rank]).astype(jnp.int32)
    order = rcv_rank ^ jnp.arange(rcv_count, dtype=jnp.int32)

    gathered = []
    for part in range(parts):
        tiles = []
        for distance in range(rcv_count):
            tile = lax.dynamic_index_in_dim(spectra, part * rcv_count + order[distance], 0, keepdims=False)
            tiles.append(tile if distance == 0 else exchange(tile, "rcv", distance))
        gathered.append(tiles)

    own_tile = gain_index.T
    line = jnp.stack([own_tile if e == 0 else exchange(own_tile, "freq", e) for e in range(freq_count)])
    near = jnp.stack([line if h == 0 else exchange(line, "rcv", 2 * h) for h in range(rcv_count // 2)])
    far = exchange(near, "rcv", 1)
    gains = pl.pallas_call(
        functools.partial(gains_kernel, source_tiles=freq_count),
        out_shape=jax.ShapeDtypeStruct((2, side, side), jnp.float32),
        in_specs=[whole_in(pltpu.SMEM), whole_in(pltpu.SMEM), whole_in(), whole_in(), whole_in()],
        out_specs=whole_in(),
        scratch_shapes=[pltpu.VMEM((senders, receiver_tile, source_tile), jnp.float32)],
        compiler_params=params(16),
        name="gains",
    )(place, gain_table, near, far, column)

    multiples = pl.pallas_call(
        functools.partial(multiples_kernel, source_tiles=freq_count),
        out_shape=jax.ShapeDtypeStruct((senders, 2, receiver_tile, source_tile), jnp.float32),
        in_specs=[whole_in(pltpu.SMEM), whole_in(pltpu.SMEM)] + [whole_in()] * (3 + rcv_count),
        out_specs=whole_in(),
        scratch_shapes=[
            pltpu.VMEM((2 * side, 2 * side), jnp.bfloat16),
            pltpu.VMEM((2 * side, 2 * side), jnp.bfloat16),
            pltpu.VMEM((side, 2 * side), jnp.bfloat16),
            pltpu.VMEM((side, 2 * side), jnp.bfloat16),
            pltpu.VMEM((side, 2 * side), jnp.float32),
            pltpu.VMEM((side, 2 * side), jnp.float32),
        ],
        compiler_params=params(40),
        name="multiples",
    )
    sender = jnp.arange(senders, dtype=jnp.int32)
    sent, received, tables = [], [], []
    for part in range(parts):
        live = (part * rcv_count + rcv_rank < own_count).astype(jnp.int32).reshape(1)
        sent.append(multiples(live, order, column, row, gains, *gathered[part]))
        bins = offsets[sender // rcv_count] + part * rcv_count + sender % rcv_count + 1
        tables.append(time_table(bins, samples).reshape(-1, samples))
        arrived = lax.all_to_all(sent[part], ("freq", "rcv"), split_axis=0, concat_axis=0, tiled=True)
        received.append(arrived.reshape(-1, source_tile))

    step = 8
    block = pl.BlockSpec((step, receiver_tile, samples), lambda n: (n, 0, 0))
    depth = tables[0].shape[0]
    base = recorded
    for part in range(parts):
        last = part == parts - 1
        if not last:
            received[part], _ = lax.optimization_barrier((received[part], sent[part + 1]))
        base = pl.pallas_call(
            functools.partial(synthesis_kernel, receiver_tile=receiver_tile, step=step),
            out_shape=(jax.ShapeDtypeStruct if last else pltpu.VMEM)(recorded.shape, jnp.float32),
            grid=(source_tile // step,),
            in_specs=[whole_in(), whole_in(), block if part == 0 else whole_in()],
            out_specs=block if last else whole_in(),
            scratch_shapes=[
                pltpu.VMEM((2 * depth // LANES, source_tile * receiver_tile, LANES), jnp.float32),
                pltpu.VMEM((3 * depth, samples), jnp.bfloat16),
            ],
            compiler_params=params(32),
            name="synthesis",
        )(received[part], tables[part], base)
        if not last:
            base = pltpu.with_memory_space_constraint(base, pltpu.VMEM)
    return base


def solution(mesh):
    placed = (P("freq", None, "rcv", None), P(), P(), P("freq", "rcv", None), P("freq", "rcv"), P())
    return jax.shard_map(
        on_device, mesh=mesh, in_specs=placed, out_specs=P("freq", "rcv", None), check_vma=False
    )
```

time: 242 us -> 230 us (0.950)
  waiting for transfers between devices: 142 us -> 89.2 us
  local copies, waits for them, and re-layouts: 10.9 us -> 26.2 us
  starting transfers between devices: 16.3 us -> 27.6 us
  between operations: 14.7 us -> 25.9 us
    all_to_all x4 -> x2, waiting for transfers between devices: 106 us -> 20.8 us  [on_device(): lax.all_to_all(sent[part], ('freq', 'rcv'), split_axis=0, concat_axis=0,...]
    ppermute x0 -> x21, waiting for transfers between devices: none -> 68.5 us  [exchange(): lax.ppermute(array, axis, [(i, i ^ distance) for i in range(lax.axis_size...]
    all_gather x1 -> x0, waiting for transfers between devices: 35.2 us -> none  [on_device(): tiles = lax.all_gather(gain_index.T, ('freq', 'rcv'), axis=0, tiled=False)]
    ppermute x0 -> x21, starting transfers between devices: none -> 21.2 us  [exchange(): lax.ppermute(array, axis, [(i, i ^ distance) for i in range(lax.axis_size...]
    unnamed x8 -> x26, local copies, waits for them, and re-layouts: 2.71 us -> 19.7 us
    all_to_all x4 -> x2, starting transfers between devices: 16.3 us -> 6.43 us  [on_device(): lax.all_to_all(sent[part], ('freq', 'rcv'), split_axis=0, concat_axis=0,...]
    slice x1, local copies, waits for them, and re-layouts: 4.95 us -> 0.67 us  [on_device(): order[distance]]
    squeeze x0 -> x1, local copies, waits for them, and re-layouts: none -> 3.95 us  [on_device(): lax.dynamic_index_in_dim(spectra, part * rcv_count + order[distance], 0,...]
  transfers between devices with their start and end apart: 5 -> 23, of which waited for: 4 -> 15; matrix products, arithmetic and copies ran while one was open for 3% -> 4% of each run, Pallas kernels for 12% -> 13%
where the time goes in v1:
time: 230 us; the launch traced here: 228 us
  waiting for transfers between devices  89.2 us (39%)
  Pallas kernels  54.4 us (24%)
  starting transfers between devices  27.6 us (12%)
  local copies, waits for them, and re-layouts  26.2 us (11%)
  between operations  25.9 us (11%)
  other arithmetic  4.35 us (2%)
    ppermute x21, waiting for transfers between devices, exchange(): lax.ppermute(array, axis, [(i, i ^ distance) for i in range(lax.axis_size...  68.5 us
    pallas_call x2, Pallas kernels, on_device(): pl.pallas_call(functools.partial(synthesis_kernel, receiver_tile=receiver...  31.4 us
    ppermute x21, starting transfers between devices, exchange(): lax.ppermute(array, axis, [(i, i ^ distance) for i in range(lax.axis_size...  21.2 us
    all_to_all x2, waiting for transfers between devices, on_device(): lax.all_to_all(sent[part], ('freq', 'rcv'), split_axis=0, concat_axis=0,...  20.8 us
    pallas_call x2, Pallas kernels, on_device(): sent.append(multiples(live, order, column, row, gains, *gathered[part]))  20.5 us
    unnamed x26, local copies, waits for them, and re-layouts  19.7 us
    all_to_all x2, starting transfers between devices, on_device(): lax.all_to_all(sent[part], ('freq', 'rcv'), split_axis=0, concat_axis=0,...  6.43 us
  transfers between devices with their start and end apart: 23, of which 15 were waited for; matrix products, arithmetic and copies ran while one was open for 4% of the time, Pallas kernels for 13%

profile of v1, /device:TPU:0, one launch (start us, length us, event | category | flops | bytes accessed | tf_op | source)
XLA Modules:
  0.0 227.6 jit_solution(5530236398209264383)
XLA Ops:
  0.0 4.0 %collective-permute-start.1 = (s32[64,128]{1,0:T(8,128)}, s32[64,128]{1,0:T(8,128)S(1)}, u32[]{:S(2)}, u32[]{:S(2)}) collective-permute-start(s32[64,128]{1,0:T(8,128)} %bitcast.77), channel_id=1, source_target_pairs={{0,16},{8,24},{16,0},{24,8},{1,17},{9,25},{17,1},{25,9},{2,18},{10... | collective-permute-start | bytes 98312 | tf_op jit(solution)/shard_map/ppermute | solution.py:173
  8.2 3.4 %collective-permute-done.2 = s32[64,128]{1,0:T(8,128)S(1)} collective-permute-done((s32[64,128]{1,0:T(8,128)}, s32[64,128]{1,0:T(8,128)S(1)}, u32[]{:S(2)}, u32[]{:S(2)}) %collective-permute-start.2) | collective-permute-done | bytes 32800 | tf_op jit(solution)/shard_map/ppermute | solution.py:173
  15.9 2.9 %collective-permute-done.4 = s32[4,64,128]{2,1,0:T(8,128)S(1)} collective-permute-done((s32[4,64,128]{2,1,0:T(8,128)S(1)}, s32[4,64,128]{2,1,0:T(8,128)S(1)}, u32[]{:S(2)}, u32[]{:S(2)}) %collective-permute-start.4) | collective-permute-done | bytes 131104 | tf_op jit(solution)/shard_map/ppermute | solution.py:173
  18.9 2.4 %collective-permute-done.5 = s32[4,64,128]{2,1,0:T(8,128)S(1)} collective-permute-done((s32[4,64,128]{2,1,0:T(8,128)S(1)}, s32[4,64,128]{2,1,0:T(8,128)S(1)}, u32[]{:S(2)}, u32[]{:S(2)}) %collective-permute-start.5) | collective-permute-done | bytes 131104 | tf_op jit(solution)/shard_map/ppermute | solution.py:173
  46.5 3.9 %dynamic-slice_bitcast_fusion = (f32[2,64,512]{2,1,0:T(8,128)S(1)}, f32[2,64,512]{2,1,0:T(8,128)S(1)}, f32[2,64,512]{2,1,0:T(8,128)}, f32[2,64,512]{2,1,0:T(8,12...) fusion(f32[16,2,64,512]{3,2,1,0:T(8,128)} %param.6, ...), kind=kLoop, calls=%fused_computation.1 | loop fusion | bytes 8388672 | tf_op jit(solution)/shard_map/jit(dynamic_index_in_dim)/squeeze | solution.py:196
  54.0 5.4 %collective-permute-done.20.refs_7_ = f32[2,64,512]{2,1,0:T(8,128)S(1)} collective-permute-done((f32[2,64,512]{2,1,0:T(8,128)S(1)}, f32[2,64,512]{2,1,0:T(8,128)S(1)}, u32[]{:S(2)}, u32[]{:S(2)}) %collective-permute-start.20) | collective-permute-done | bytes 262176 | tf_op jit(solution)/shard_map/ppermute | solution.py:173
  60.7 4.9 %collective-permute-done.18.refs_5_ = f32[2,64,512]{2,1,0:T(8,128)S(1)} collective-permute-done((f32[2,64,512]{2,1,0:T(8,128)S(1)}, f32[2,64,512]{2,1,0:T(8,128)S(1)}, u32[]{:S(2)}, u32[]{:S(2)}) %collective-permute-start.18) | collective-permute-done | bytes 262176 | tf_op jit(solution)/shard_map/ppermute | solution.py:173
  71.3 2.5 %gains.1.gains_ref = f32[2,512,512]{2,1,0:T(8,128)S(1)} custom-call(s32[2]{0:T(128)S(1)} %pad_add_fusion.2.place_ref, f32[2,16]{1,0:T(2,128)S(1)} %copy-done.11, s32[4,4,64,128]{3,2,1,0:T(8,128)S(1)} %pad_add_fusion.near_ref, s32[4,4,64,128]{3,2,1,0:T(8,128)S(1)} %copy-done.5, s32[512,1]{1,0:T(8,128)S(1)} %copy.11.column_ref), custom_call_target="tpu_custom_call" | custom-call | tf_op jit(solution)/shard_map/gains/pallas_call | solution.py:204
  73.8 3.2 %collective-permute-done.19.refs_6_ = f32[2,64,512]{2,1,0:T(8,128)} collective-permute-done((f32[2,64,512]{2,1,0:T(8,128)}, f32[2,64,512]{2,1,0:T(8,128)}, u32[]{:S(2)}, u32[]{:S(2)}) %collective-permute-start.19) | collective-permute-done | bytes 262176 | tf_op jit(solution)/shard_map/ppermute | solution.py:173
  78.9 10.2 %multiples.3 = f32[32,2,64,128]{3,2,1,0:T(8,128)S(1)} custom-call(s32[1]{0:T(128)} %bitcast.39.live_ref, s32[8]{0:T(128)S(1)} %iota_xor_fusion.order_ref, s32[512,1]{1,0:T(8,128)S(1)} %copy.11.column_ref, s32[1,512]{1,0:T(1,128)S(1)} %bitcast.72, f32[2,512,512]{2,1,0:T(8,128)S(1)} %gains.1.gains_ref, f32[2,64,512]{2,1,0:T(8,128)S(1)} %get-tuple-element.15.refs_0_, ...), custom_call_target="tpu_custom_call" | custom-call | tf_op jit(solution)/shard_map/multiples/pallas_call | solution.py:234
  90.5 3.5 %all-to-all-start.1 = ((f32[32,2,64,128]{3,2,1,0:T(8,128)}), f32[32,2,64,128]{3,2,1,0:T(8,128)}, u32[]{:S(2)}, u32[]{:S(2)}) async-start(f32[32,2,64,128]{3,2,1,0:T(8,128)} %copy-done.2), calls=%async_computation.1 | async-start | bytes 4194304 | tf_op jit(solution)/shard_map/all_to_all | solution.py:237
  93.9 2.3 %collective-permute-start.13 = (f32[2,64,512]{2,1,0:T(8,128)}, f32[2,64,512]{2,1,0:T(8,128)S(1)}, u32[]{:S(2)}, u32[]{:S(2)}) collective-permute-start(f32[2,64,512]{2,1,0:T(8,128)} %get-tuple-element.16), channel_id=1, source_target_pairs={{0,7},{1,6},{2,5},{3,4},{4,3},{5,2},{6,1},{7,0},{8,15},{9,14},{10,... | collective-permute-start | bytes 786440 | tf_op jit(solution)/shard_map/ppermute | solution.py:173
  99.7 22.6 %collective-permute-done.13.refs_7_ = f32[2,64,512]{2,1,0:T(8,128)S(1)} collective-permute-done((f32[2,64,512]{2,1,0:T(8,128)}, f32[2,64,512]{2,1,0:T(8,128)S(1)}, u32[]{:S(2)}, u32[]{:S(2)}) %collective-permute-start.13) | collective-permute-done | bytes 262176 | tf_op jit(solution)/shard_map/ppermute | solution.py:173
  122.6 7.7 %collective-permute-done.12.refs_6_ = f32[2,64,512]{2,1,0:T(8,128)S(1)} collective-permute-done((f32[2,64,512]{2,1,0:T(8,128)}, f32[2,64,512]{2,1,0:T(8,128)S(1)}, u32[]{:S(2)}, u32[]{:S(2)}) %collective-permute-start.12) | collective-permute-done | bytes 262176 | tf_op jit(solution)/shard_map/ppermute | solution.py:173
  133.1 8.5 %collective-permute-done.10.refs_4_ = f32[2,64,512]{2,1,0:T(8,128)} collective-permute-done((f32[2,64,512]{2,1,0:T(8,128)}, f32[2,64,512]{2,1,0:T(8,128)}, u32[]{:S(2)}, u32[]{:S(2)}) %collective-permute-start.10) | collective-permute-done | bytes 262176 | tf_op jit(solution)/shard_map/ppermute | solution.py:173
  141.6 2.7 %collective-permute-done.8.refs_2_ = f32[2,64,512]{2,1,0:T(8,128)} collective-permute-done((f32[2,64,512]{2,1,0:T(8,128)}, f32[2,64,512]{2,1,0:T(8,128)}, u32[]{:S(2)}, u32[]{:S(2)}) %collective-permute-start.8) | collective-permute-done | bytes 262176 | tf_op jit(solution)/shard_map/ppermute | solution.py:173
  144.3 10.3 %multiples.2 = f32[32,2,64,128]{3,2,1,0:T(8,128)S(1)} custom-call(s32[1]{0:T(128)} %bitcast.1.live_ref, s32[8]{0:T(128)S(1)} %iota_xor_fusion.order_ref, s32[512,1]{1,0:T(8,128)S(1)} %copy.11.column_ref, s32[1,512]{1,0:T(1,128)S(1)} %bitcast.73, f32[2,512,512]{2,1,0:T(8,128)S(1)} %gains.1.gains_ref, f32[2,64,512]{2,1,0:T(8,128)S(1)} %get-tuple-element.23.refs_0_, ...), custom_call_target="tpu_custom_call" | custom-call | tf_op jit(solution)/shard_map/multiples/pallas_call | solution.py:234
  156.0 2.9 %all-to-all-start = ((f32[32,2,64,128]{3,2,1,0:T(8,128)}), f32[32,2,64,128]{3,2,1,0:T(8,128)S(1)}, u32[]{:S(2)}, u32[]{:S(2)}) async-start(f32[32,2,64,128]{3,2,1,0:T(8,128)} %copy-done.3), calls=%async_computation | async-start | bytes 4194304 | tf_op jit(solution)/shard_map/all_to_all | solution.py:237
  159.8 2.6 %add_add_fusion = (s32[32]{0:T(128)S(1)}, s32[32]{0:T(128)S(1)}) fusion(s32[]{:T(128)} %bitcast.37, s32[]{:T(128)} %bitcast.36, s32[]{:T(128)} %bitcast.35, s32[]{:T(128)} %bitcast.34), kind=kLoop, calls=%fused_computation.54 | loop fusion | flops 800 | bytes 272 | tf_op jit(solution)/shard_map/add | solution.py:235
  163.5 17.4 %synthesis.2.base_ref = f32[128,64,512]{2,1,0:T(8,128)S(1)} custom-call(f32[4096,128]{1,0:T(8,128)} %bitcast.48.coef_ref, f32[64,512]{1,0:T(8,128)S(1)} %reshape.312.table_ref, f32[128,64,512]{2,1,0:T(8,128)} %base_ref.1), custom_call_target="tpu_custom_call" | custom-call | tf_op jit(solution)/shard_map/synthesis/pallas_call | solution.py:248
  180.9 6.2 %copy-done = f32[128,64,512]{2,1,0:T(8,128)} copy-done((f32[128,64,512]{2,1,0:T(8,128)}, f32[128,64,512]{2,1,0:T(8,128)S(1)}, u32[]{:S(2)}) %copy-start) | copy-done | bytes 16777240
  187.1 20.8 %all-to-all-done = f32[32,2,64,128]{3,2,1,0:T(8,128)S(1)} async-done(((f32[32,2,64,128]{3,2,1,0:T(8,128)}), f32[32,2,64,128]{3,2,1,0:T(8,128)S(1)}, u32[]{:S(2)}, u32[]{:S(2)}) %all-to-all-start) | async-done | bytes 2097184 | tf_op jit(solution)/shard_map/all_to_all | solution.py:237
  207.9 5.8 %copy-done.1 = f32[128,64,512]{2,1,0:T(8,128)S(1)} copy-done((f32[128,64,512]{2,1,0:T(8,128)S(1)}, f32[128,64,512]{2,1,0:T(8,128)}, u32[]{:S(2)}) %copy-start.1) | copy-done | bytes 16777240
  213.6 14.0 %synthesis.3 = f32[128,64,512]{2,1,0:T(8,128)} custom-call(f32[4096,128]{1,0:T(8,128)S(1)} %bitcast.70, f32[64,512]{1,0:T(8,128)S(1)} %reshape.308.table_ref, f32[128,64,512]{2,1,0:T(8,128)S(1)} %copy-done.1), custom_call_target="tpu_custom_call" | custom-call | tf_op jit(solution)/shard_map/synthesis/pallas_call | solution.py:248
  (74 shorter events, 31.7 us)
Async XLA Ops:
  0.0 6.6 %collective-permute-start.1 = (s32[64,128]{1,0:T(8,128)}, s32[64,128]{1,0:T(8,128)S(1)}, u32[]{:S(2)}, u32[]{:S(2)}) collective-permute-start(s32[64,128]{1,0:T(8,128)} %bitcast.77), channel_id=1, source_target_pairs={{0,16},{8,24},{16,0},{24,8},{1,17},{9,25},{17,1},{25,9},{2,18},{10... | collective-permute-start | bytes 98312 | tf_op jit(solution)/shard_map/ppermute | solution.py:173
  4.0 4.1 %collective-permute-start = (s32[64,128]{1,0:T(8,128)}, s32[64,128]{1,0:T(8,128)S(1)}, u32[]{:S(2)}, u32[]{:S(2)}) collective-permute-start(s32[64,128]{1,0:T(8,128)} %bitcast.78), channel_id=1, source_target_pairs={{0,8},{8,0},{16,24},{24,16},{1,9},{9,1},{17,25},{25,17},{2,10},{10... | collective-permute-start | bytes 98312 | tf_op jit(solution)/shard_map/ppermute | solution.py:173
  5.6 5.9 %collective-permute-start.2 = (s32[64,128]{1,0:T(8,128)}, s32[64,128]{1,0:T(8,128)S(1)}, u32[]{:S(2)}, u32[]{:S(2)}) collective-permute-start(s32[64,128]{1,0:T(8,128)} %bitcast.79), channel_id=1, source_target_pairs={{0,24},{8,16},{16,8},{24,0},{1,25},{9,17},{17,9},{25,1},{2,26},{10... | collective-permute-start | bytes 98312 | tf_op jit(solution)/shard_map/ppermute | solution.py:173
  12.3 6.4 %collective-permute-start.4 = (s32[4,64,128]{2,1,0:T(8,128)S(1)}, s32[4,64,128]{2,1,0:T(8,128)S(1)}, u32[]{:S(2)}, u32[]{:S(2)}) collective-permute-start(s32[4,64,128]{2,1,0:T(8,128)S(1)} %get-tuple-element.26), channel_id=1, source_target_pairs={{0,4},{1,5},{2,6},{3,7},{4,0},{5,1},{6,2},{7,3},{8,12},{9,13},{10,... | collective-permute-start | bytes 393224 | tf_op jit(solution)/shard_map/ppermute | solution.py:173
  13.9 5.0 %collective-permute-start.3 = (s32[4,64,128]{2,1,0:T(8,128)S(1)}, s32[4,64,128]{2,1,0:T(8,128)S(1)}, u32[]{:S(2)}, u32[]{:S(2)}) collective-permute-start(s32[4,64,128]{2,1,0:T(8,128)S(1)} %get-tuple-element.26), channel_id=1, source_target_pairs={{0,2},{1,3},{2,0},{3,1},{4,6},{5,7},{6,4},{7,5},{8,10},{9,11},{10,... | collective-permute-start | bytes 393224 | tf_op jit(solution)/shard_map/ppermute | solution.py:173
  15.4 5.9 %collective-permute-start.5 = (s32[4,64,128]{2,1,0:T(8,128)S(1)}, s32[4,64,128]{2,1,0:T(8,128)S(1)}, u32[]{:S(2)}, u32[]{:S(2)}) collective-permute-start(s32[4,64,128]{2,1,0:T(8,128)S(1)} %get-tuple-element.26), channel_id=1, source_target_pairs={{0,6},{1,7},{2,4},{3,5},{4,2},{5,3},{6,0},{7,1},{8,14},{9,15},{10,... | collective-permute-start | bytes 393224 | tf_op jit(solution)/shard_map/ppermute | solution.py:173
  21.3 45.2 %collective-permute-start.6 = (s32[4,4,64,128]{3,2,1,0:T(8,128)S(1)}, s32[4,4,64,128]{3,2,1,0:T(8,128)S(1)}, u32[]{:S(2)}, u32[]{:S(2)}) collective-permute-start(s32[4,4,64,128]{3,2,1,0:T(8,128)S(1)} %pad_add_fusion.near_ref), channel_id=1, source_target_pairs={{0,1},{1,0},{2,3},{3,2},{4,5},{5,4},{6,7},{7,6},{8,9},{9,8},{10,11... | collective-permute-start | bytes 1572872 | tf_op jit(solution)/shard_map/ppermute | solution.py:173
  46.5 23.8 %copy-start.11 = (f32[2,16]{1,0:T(2,128)S(1)}, f32[2,16]{1,0:T(2,128)}, u32[]{:S(2)}) copy-start(f32[2,16]{1,0:T(2,128)} %table_ref.1) | copy-start | bytes 388
  50.4 9.0 %collective-permute-start.20 = (f32[2,64,512]{2,1,0:T(8,128)S(1)}, f32[2,64,512]{2,1,0:T(8,128)S(1)}, u32[]{:S(2)}, u32[]{:S(2)}) collective-permute-start(f32[2,64,512]{2,1,0:T(8,128)S(1)} %get-tuple-element.9), channel_id=1, source_target_pairs={{0,7},{1,6},{2,5},{3,4},{4,3},{5,2},{6,1},{7,0},{8,15},{9,14},{10,... | collective-permute-start | bytes 786440 | tf_op jit(solution)/shard_map/ppermute | solution.py:173
  52.0 13.6 %collective-permute-start.18 = (f32[2,64,512]{2,1,0:T(8,128)S(1)}, f32[2,64,512]{2,1,0:T(8,128)S(1)}, u32[]{:S(2)}, u32[]{:S(2)}) collective-permute-start(f32[2,64,512]{2,1,0:T(8,128)S(1)} %get-tuple-element.10), channel_id=1, source_target_pairs={{0,5},{1,4},{2,7},{3,6},{4,1},{5,0},{6,3},{7,2},{8,13},{9,12},{10,... | collective-permute-start | bytes 786440 | tf_op jit(solution)/shard_map/ppermute | solution.py:173
  52.2 21.6 %collective-permute-start.17 = (f32[2,64,512]{2,1,0:T(8,128)}, f32[2,64,512]{2,1,0:T(8,128)}, u32[]{:S(2)}, u32[]{:S(2)}) collective-permute-start(f32[2,64,512]{2,1,0:T(8,128)} %get-tuple-element.11), channel_id=1, source_target_pairs={{0,4},{1,5},{2,6},{3,7},{4,0},{5,1},{6,2},{7,3},{8,12},{9,13},{10,... | collective-permute-start | bytes 786440 | tf_op jit(solution)/shard_map/ppermute | solution.py:173
  53.6 20.2 %collective-permute-start.16 = (f32[2,64,512]{2,1,0:T(8,128)}, f32[2,64,512]{2,1,0:T(8,128)}, u32[]{:S(2)}, u32[]{:S(2)}) collective-permute-start(f32[2,64,512]{2,1,0:T(8,128)} %get-tuple-element.12), channel_id=1, source_target_pairs={{0,3},{1,2},{2,1},{3,0},{4,7},{5,6},{6,5},{7,4},{8,11},{9,10},{10,... | collective-permute-start | bytes 786440 | tf_op jit(solution)/shard_map/ppermute | solution.py:173
  60.2 13.7 %collective-permute-start.15 = (f32[2,64,512]{2,1,0:T(8,128)}, f32[2,64,512]{2,1,0:T(8,128)}, u32[]{:S(2)}, u32[]{:S(2)}) collective-permute-start(f32[2,64,512]{2,1,0:T(8,128)} %get-tuple-element.13), channel_id=1, source_target_pairs={{0,2},{1,3},{2,0},{3,1},{4,6},{5,7},{6,4},{7,5},{8,10},{9,11},{10,... | collective-permute-start | bytes 786440 | tf_op jit(solution)/shard_map/ppermute | solution.py:173
  66.3 7.5 %collective-permute-start.14 = (f32[2,64,512]{2,1,0:T(8,128)}, f32[2,64,512]{2,1,0:T(8,128)}, u32[]{:S(2)}, u32[]{:S(2)}) collective-permute-start(f32[2,64,512]{2,1,0:T(8,128)} %get-tuple-element.14), channel_id=1, source_target_pairs={{0,1},{1,0},{2,3},{3,2},{4,5},{5,4},{6,7},{7,6},{8,9},{9,8},{10,11... | collective-permute-start | bytes 786440 | tf_op jit(solution)/shard_map/ppermute | solution.py:173
  67.3 9.7 %collective-permute-start.19 = (f32[2,64,512]{2,1,0:T(8,128)}, f32[2,64,512]{2,1,0:T(8,128)}, u32[]{:S(2)}, u32[]{:S(2)}) collective-permute-start(f32[2,64,512]{2,1,0:T(8,128)} %get-tuple-element.24), channel_id=1, source_target_pairs={{0,6},{1,7},{2,4},{3,5},{4,2},{5,3},{6,0},{7,1},{8,14},{9,15},{10,... | collective-permute-start | bytes 786440 | tf_op jit(solution)/shard_map/ppermute | solution.py:173
  90.5 65.5 %all-to-all-start.1 = ((f32[32,2,64,128]{3,2,1,0:T(8,128)}), f32[32,2,64,128]{3,2,1,0:T(8,128)}, u32[]{:S(2)}, u32[]{:S(2)}) async-start(f32[32,2,64,128]{3,2,1,0:T(8,128)} %copy-done.2), calls=%async_computation.1 | async-start | bytes 4194304 | tf_op jit(solution)/shard_map/all_to_all | solution.py:237
  93.9 28.3 %collective-permute-start.13 = (f32[2,64,512]{2,1,0:T(8,128)}, f32[2,64,512]{2,1,0:T(8,128)S(1)}, u32[]{:S(2)}, u32[]{:S(2)}) collective-permute-start(f32[2,64,512]{2,1,0:T(8,128)} %get-tuple-element.16), channel_id=1, source_target_pairs={{0,7},{1,6},{2,5},{3,4},{4,3},{5,2},{6,1},{7,0},{8,15},{9,14},{10,... | collective-permute-start | bytes 786440 | tf_op jit(solution)/shard_map/ppermute | solution.py:173
  96.3 34.1 %collective-permute-start.12 = (f32[2,64,512]{2,1,0:T(8,128)}, f32[2,64,512]{2,1,0:T(8,128)S(1)}, u32[]{:S(2)}, u32[]{:S(2)}) collective-permute-start(f32[2,64,512]{2,1,0:T(8,128)} %get-tuple-element.17), channel_id=1, source_target_pairs={{0,6},{1,7},{2,4},{3,5},{4,2},{5,3},{6,0},{7,1},{8,14},{9,15},{10,... | collective-permute-start | bytes 786440 | tf_op jit(solution)/shard_map/ppermute | solution.py:173
  96.6 36.5 %collective-permute-start.11 = (f32[2,64,512]{2,1,0:T(8,128)}, f32[2,64,512]{2,1,0:T(8,128)S(1)}, u32[]{:S(2)}, u32[]{:S(2)}) collective-permute-start(f32[2,64,512]{2,1,0:T(8,128)} %get-tuple-element.18), channel_id=1, source_target_pairs={{0,5},{1,4},{2,7},{3,6},{4,1},{5,0},{6,3},{7,2},{8,13},{9,12},{10,... | collective-permute-start | bytes 786440 | tf_op jit(solution)/shard_map/ppermute | solution.py:173
  98.0 43.7 %collective-permute-start.10 = (f32[2,64,512]{2,1,0:T(8,128)}, f32[2,64,512]{2,1,0:T(8,128)}, u32[]{:S(2)}, u32[]{:S(2)}) collective-permute-start(f32[2,64,512]{2,1,0:T(8,128)} %get-tuple-element.19), channel_id=1, source_target_pairs={{0,4},{1,5},{2,6},{3,7},{4,0},{5,1},{6,2},{7,3},{8,12},{9,13},{10,... | collective-permute-start | bytes 786440 | tf_op jit(solution)/shard_map/ppermute | solution.py:173
  98.4 43.2 %collective-permute-start.9 = (f32[2,64,512]{2,1,0:T(8,128)}, f32[2,64,512]{2,1,0:T(8,128)}, u32[]{:S(2)}, u32[]{:S(2)}) collective-permute-start(f32[2,64,512]{2,1,0:T(8,128)} %get-tuple-element.20), channel_id=1, source_target_pairs={{0,3},{1,2},{2,1},{3,0},{4,7},{5,6},{6,5},{7,4},{8,11},{9,10},{10,... | collective-permute-start | bytes 786440 | tf_op jit(solution)/shard_map/ppermute | solution.py:173
  122.3 22.0 %collective-permute-start.8 = (f32[2,64,512]{2,1,0:T(8,128)}, f32[2,64,512]{2,1,0:T(8,128)}, u32[]{:S(2)}, u32[]{:S(2)}) collective-permute-start(f32[2,64,512]{2,1,0:T(8,128)} %get-tuple-element.21), channel_id=1, source_target_pairs={{0,2},{1,3},{2,0},{3,1},{4,6},{5,7},{6,4},{7,5},{8,10},{9,11},{10,... | collective-permute-start | bytes 786440 | tf_op jit(solution)/shard_map/ppermute | solution.py:173
  130.4 13.9 %collective-permute-start.7 = (f32[2,64,512]{2,1,0:T(8,128)}, f32[2,64,512]{2,1,0:T(8,128)}, u32[]{:S(2)}, u32[]{:S(2)}) collective-permute-start(f32[2,64,512]{2,1,0:T(8,128)} %get-tuple-element.22), channel_id=1, source_target_pairs={{0,1},{1,0},{2,3},{3,2},{4,5},{5,4},{6,7},{7,6},{8,9},{9,8},{10,11... | collective-permute-start | bytes 786440 | tf_op jit(solution)/shard_map/ppermute | solution.py:173
  156.0 51.9 %all-to-all-start = ((f32[32,2,64,128]{3,2,1,0:T(8,128)}), f32[32,2,64,128]{3,2,1,0:T(8,128)S(1)}, u32[]{:S(2)}, u32[]{:S(2)}) async-start(f32[32,2,64,128]{3,2,1,0:T(8,128)} %copy-done.3), calls=%async_computation | async-start | bytes 4194304 | tf_op jit(solution)/shard_map/all_to_all | solution.py:237
  (12 other events, 65.6 us)

commit v2 on v1

--- a/solution.py
+++ b/solution.py
@@ -66,12 +66,24 @@
             out_ref[1, rows, cols] = second
 
 
-def multiples_kernel(live_ref, order_ref, column_ref, row_ref, gains_ref, *refs, source_tiles):
-    data, (out_ref, wh, wl, uh, ul, y1, y2) = refs[:-7], refs[-7:]
-    receiver_tiles = len(data)
-    _, receiver_tile, side = data[0].shape
+def pack_kernel(spectra_ref, *refs, first_slot):
+    outs, sems = refs[:-1], refs[-1]
+    rank = lax.axis_index("rcv")
+    copies = [
+        pltpu.make_async_copy(spectra_ref.at[first_slot + (rank ^ (n + 1))], out, sems.at[n]) for n, out in enumerate(outs)
+    ]
+    for copy in copies:
+        copy.start()
+    for copy in copies:
+        copy.wait()
+
+
+def multiples_kernel(live_ref, column_ref, row_ref, spectra_ref, gains_hbm, *refs, source_tiles, first_slot):
+    tiles, (out_ref, data, gains, u, w, y1, y2, tile_sems, gain_sem) = refs[:-9], refs[-9:]
+    receiver_tiles, _, receiver_tile, side = data.shape
     source_tile = side // source_tiles
     pick = min(PICK, side)
+    rank = lax.axis_index("rcv")
 
     @pl.when(live_ref[0] == 0)
     def _():
@@ -79,51 +91,59 @@
 
     @pl.when(live_ref[0] != 0)
     def _():
-        for i in range(receiver_tiles):
-            first_row = pl.multiple_of(order_ref[i] * receiver_tile, receiver_tile)
-            top = pl.ds(first_row, receiver_tile)
-            low = pl.ds(side + first_row, receiver_tile)
-            real_high, real_low = split(data[i][0])
-            imag_high, imag_low = split(data[i][1])
-            wh[top, :side] = real_high
-            wh[low, side:] = real_high
-            wh[top, side:] = imag_high
-            wh[low, :side] = -imag_high
-            wl[top, :side] = real_low
-            wl[low, side:] = real_low
-            wl[top, side:] = imag_low
-            wl[low, :side] = -imag_low
+        sources = [spectra_ref.at[first_slot + rank]] + list(tiles)
+        copies = [pltpu.make_async_copy(source, data.at[n], tile_sems.at[n]) for n, source in enumerate(sources)]
+        for copy in copies:
+            copy.start()
+        gain_copy = pltpu.make_async_copy(gains_hbm, gains, gain_sem)
+        gain_copy.start()
+        for n, copy in enumerate(copies):
+            copy.wait()
+            first_row = (rank ^ n) * receiver_tile
+            real, imag = split(data[n, 0]), split(data[n, 1])
+            for place, part in ((0, 0), (1, 1), (2, 0)):
+                top = pl.ds(pl.multiple_of(first_row + place * 2 * side, receiver_tile), receiver_tile)
+                low = pl.ds(pl.multiple_of(first_row + (place * 2 + 1) * side, receiver_tile), receiver_tile)
+                w[top, :side] = real[part]
+                w[top, side:] = imag[part]
+                w[low, :side] = -imag[part]
+                w[low, side:] = real[part]
+        high, again, low = (slice(n * 2 * side, (n + 1) * 2 * side) for n in range(3))
         for start in range(0, side, pick):
             rows = slice(start, start + pick)
             table = gather_table(column_ref[rows, :], start, pick)
-            uh[rows, :] = mm(table, wh[rows, :]).astype(jnp.bfloat16)
-            ul[rows, :] = mm(table, wl[rows, :]).astype(jnp.bfloat16)
+            u[rows, high] = mm(table, w[rows, :]).astype(jnp.bfloat16)
+            u[rows, again] = u[rows, high]
+            u[rows, low] = mm(table, w[2 * side + start : 2 * side + start + pick, :]).astype(jnp.bfloat16)
 
         def product(result):
             for start in range(0, 2 * side, PICK):
                 cols = slice(start, start + PICK)
-                result[:, cols] = mm(uh[...], wh[:, cols]) + mm(uh[...], wl[:, cols]) + mm(ul[...], wh[:, cols])
+                result[:, cols] = mm(u[...], w[:, cols])
 
         product(y1)
         for start in range(0, side, 64):
             rows = slice(start, start + 64)
-            uh[rows, :], ul[rows, :] = split(y1[rows, :])
+            u[rows, high], u[rows, low] = split(y1[rows, :])
+            u[rows, again] = u[rows, high]
         product(y2)
+        gain_copy.wait()
         block = 128
         for q in range(0, side, block):
             for s in range(0, side, block):
                 qs, ss = slice(q, q + block), slice(s, s + block)
-                first_gain, second_gain = gains_ref[0, qs, ss], gains_ref[1, qs, ss]
+                first_gain, second_gain = gains[0, qs, ss], gains[1, qs, ss]
                 for c in range(2):
                     qc, sc = slice(c * side + q, c * side + q + block), slice(c * side + s, c * side + s + block)
                     value = first_gain * (y1[qs, sc] + y1[ss, qc].T) + second_gain * (y2[qs, sc] + y2[ss, qc].T)
-                    uh[qs, sc], ul[qs, sc] = split(value)
+                    u[qs, sc], u[qs, 2 * side + c * side + s : 2 * side + c * side + s + block] = split(value)
         for start in range(0, side, pick):
             rows = slice(start, start + pick)
             table = scatter_table(row_ref[:, rows], start, pick)
             for c in range(2):
-                cols = slice(c * side, (c + 1) * side)
-                natural = mm(table, uh[rows, cols]) + mm(table, ul[rows, cols])
+                natural = mm(table, u[rows, c * side : (c + 1) * side]) + mm(
+                    table, u[rows, (2 + c) * side : (3 + c) * side]
+                )
                 for i in range(pick // receiver_tile):
                     tile = start // receiver_tile + i
                     for a in range(source_tiles):
@@ -132,12 +152,15 @@
                         ]
 
 
-def synthesis_kernel(coef_ref, table_ref, base_ref, out_ref, lines, tables, *, receiver_tile, step):
+def synthesis_kernel(table_ref, coef_hbm, base_ref, out_ref, coef_ref, lines, tables, sem, *, receiver_tile, step):
     depth = table_ref.shape[0]
     source_tile = coef_ref.shape[1]
 
     @pl.when(pl.program_id(0) == 0)
     def _():
+        copy = pltpu.make_async_copy(coef_hbm, coef_ref, sem)
+        copy.start()
+        copy.wait()
         for r in range(receiver_tile):
             column = coef_ref[pl.ds(r, depth, stride=receiver_tile), :]
             high = column.astype(jnp.bfloat16).astype(jnp.float32)
@@ -154,11 +177,7 @@
     both = jnp.concatenate([lines[g, rows, :] for g in range(lines.shape[0])], axis=1).astype(jnp.bfloat16)
     total = mm(jnp.concatenate([both, both[:, :depth]], axis=1), tables[...])
 
-    def mine(ref):
-        whole = ref.shape[0] != step
-        return pl.ds(pl.multiple_of(pl.program_id(0) * step, step), step) if whole else slice(None)
-
-    out_ref[mine(out_ref)] = base_ref[mine(base_ref)] - total.reshape(step, receiver_tile, -1)
+    out_ref[...] = base_ref[...] - total.reshape(base_ref.shape)
 
 
 def params(mebibytes):
@@ -187,18 +206,24 @@
     column = partner[:, None]
     row = partner[None, :]
     place = jnp.stack([freq_rank, rcv_rank]).astype(jnp.int32)
-    order = rcv_rank ^ jnp.arange(rcv_count, dtype=jnp.int32)
+    hbm = whole_in(pltpu.HBM)
 
     gathered = []
     for part in range(parts):
-        tiles = []
-        for distance in range(rcv_count):
-            tile = lax.dynamic_index_in_dim(spectra, part * rcv_count + order[distance], 0, keepdims=False)
-            tiles.append(tile if distance == 0 else exchange(tile, "rcv", distance))
-        gathered.append(tiles)
+        tile = pltpu.HBM(spectra.shape[1:], spectra.dtype)
+        packed = pl.pallas_call(
+            functools.partial(pack_kernel, first_slot=part * rcv_count),
+            out_shape=[tile] * (rcv_count - 1),
+            in_specs=[hbm],
+            out_specs=[hbm] * (rcv_count - 1),
+            scratch_shapes=[pltpu.SemaphoreType.DMA((rcv_count - 1,))],
+            name="pack",
+        )(spectra)
+        gathered.append([exchange(tile, "rcv", n + 1) for n, tile in enumerate(packed)])
 
     own_tile = gain_index.T
     line = jnp.stack([own_tile if e == 0 else exchange(own_tile, "freq", e) for e in range(freq_count)])
+    line, gathered[0][0] = lax.optimization_barrier((line, gathered[0][0]))
     near = jnp.stack([line if h == 0 else exchange(line, "rcv", 2 * h) for h in range(rcv_count // 2)])
     far = exchange(near, "rcv", 1)
     gains = pl.pallas_call(
@@ -211,55 +236,56 @@
         name="gains",
     )(place, gain_table, near, far, column)
 
-    multiples = pl.pallas_call(
-        functools.partial(multiples_kernel, source_tiles=freq_count),
-        out_shape=jax.ShapeDtypeStruct((senders, 2, receiver_tile, source_tile), jnp.float32),
-        in_specs=[whole_in(pltpu.SMEM), whole_in(pltpu.SMEM)] + [whole_in()] * (3 + rcv_count),
-        out_specs=whole_in(),
-        scratch_shapes=[
-            pltpu.VMEM((2 * side, 2 * side), jnp.bfloat16),
-            pltpu.VMEM((2 * side, 2 * side), jnp.bfloat16),
-            pltpu.VMEM((side, 2 * side), jnp.bfloat16),
-            pltpu.VMEM((side, 2 * side), jnp.bfloat16),
-            pltpu.VMEM((side, 2 * side), jnp.float32),
-            pltpu.VMEM((side, 2 * side), jnp.float32),
-        ],
-        compiler_params=params(40),
-        name="multiples",
-    )
     sender = jnp.arange(senders, dtype=jnp.int32)
     sent, received, tables = [], [], []
     for part in range(parts):
         live = (part * rcv_count + rcv_rank < own_count).astype(jnp.int32).reshape(1)
-        sent.append(multiples(live, order, column, row, gains, *gathered[part]))
+        multiples = pl.pallas_call(
+            functools.partial(multiples_kernel, source_tiles=freq_count, first_slot=part * rcv_count),
+            out_shape=jax.ShapeDtypeStruct((senders, 2, receiver_tile, source_tile), jnp.float32),
+            in_specs=[whole_in(pltpu.SMEM), whole_in(), whole_in()] + [hbm] * (1 + rcv_count),
+            out_specs=whole_in(),
+            scratch_shapes=[
+                pltpu.VMEM((rcv_count, 2, receiver_tile, side), jnp.float32),
+                pltpu.VMEM((2, side, side), jnp.float32),
+                pltpu.VMEM((side, 6 * side), jnp.bfloat16),
+                pltpu.VMEM((6 * side, 2 * side), jnp.bfloat16),
+                pltpu.VMEM((side, 2 * side), jnp.float32),
+                pltpu.VMEM((side, 2 * side), jnp.float32),
+                pltpu.SemaphoreType.DMA((rcv_count,)),
+                pltpu.SemaphoreType.DMA,
+            ],
+            compiler_params=params(48),
+            name="multiples",
+        )
+        sent.append(multiples(live, column, row, spectra, gains, *gathered[part]))
         bins = offsets[sender // rcv_count] + part * rcv_count + sender % rcv_count + 1
         tables.append(time_table(bins, samples).reshape(-1, samples))
         arrived = lax.all_to_all(sent[part], ("freq", "rcv"), split_axis=0, concat_axis=0, tiled=True)
         received.append(arrived.reshape(-1, source_tile))
 
-    step = 8
+    step = 16
     block = pl.BlockSpec((step, receiver_tile, samples), lambda n: (n, 0, 0))
     depth = tables[0].shape[0]
     base = recorded
     for part in range(parts):
-        last = part == parts - 1
-        if not last:
+        if part < parts - 1:
             received[part], _ = lax.optimization_barrier((received[part], sent[part + 1]))
         base = pl.pallas_call(
             functools.partial(synthesis_kernel, receiver_tile=receiver_tile, step=step),
-            out_shape=(jax.ShapeDtypeStruct if last else pltpu.VMEM)(recorded.shape, jnp.float32),
+            out_shape=jax.ShapeDtypeStruct(recorded.shape, jnp.float32),
             grid=(source_tile // step,),
-            in_specs=[whole_in(), whole_in(), block if part == 0 else whole_in()],
-            out_specs=block if last else whole_in(),
+            in_specs=[whole_in(), hbm, block],
+            out_specs=block,
             scratch_shapes=[
+                pltpu.VMEM((depth * receiver_tile, source_tile), jnp.float32),
                 pltpu.VMEM((2 * depth // LANES, source_tile * receiver_tile, LANES), jnp.float32),
                 pltpu.VMEM((3 * depth, samples), jnp.bfloat16),
+                pltpu.SemaphoreType.DMA,
             ],
-            compiler_params=params(32),
+            compiler_params=params(48),
             name="synthesis",
-        )(received[part], tables[part], base)
-        if not last:
-            base = pltpu.with_memory_space_constraint(base, pltpu.VMEM)
+        )(tables[part], received[part], base)
     return base
 
 

time: 230 us -> 289 us (1.26)
  Pallas kernels: 54.4 us -> 177 us
  between operations: 25.9 us -> 1.67 us
  local copies, waits for them, and re-layouts: 26.2 us -> 5.77 us
  waiting for transfers between devices: 89.2 us -> 71.6 us
    pallas_call x2 -> x4, Pallas kernels: 20.5 us -> 135 us  [the longest x2 114 us: on_device(): pl.pallas_call(functools.partial(pack_kernel, first_slot=part * rcv_count...]
    ppermute x21, waiting for transfers between devices: 68.5 us -> 45.7 us  [exchange(): lax.ppermute(array, axis, [(i, i ^ distance) for i in range(lax.axis_size...]
    unnamed x26 -> x14, local copies, waits for them, and re-layouts: 19.7 us -> 3.98 us
    pallas_call x2, Pallas kernels: 31.4 us -> 38.7 us  [on_device(): pl.pallas_call(functools.partial(synthesis_kernel, receiver_tile=receiver...]
    all_to_all x2, waiting for transfers between devices: 20.8 us -> 25.9 us  [on_device(): lax.all_to_all(sent[part], ('freq', 'rcv'), split_axis=0, concat_axis=0,...]
    squeeze x1 -> x0, local copies, waits for them, and re-layouts: 3.95 us -> none  [on_device(): lax.dynamic_index_in_dim(spectra, part * rcv_count + order[distance], 0,...]
  transfers between devices with their start and end apart: 23 -> 23, of which waited for: 15 -> 11; matrix products, arithmetic and copies ran while one was open for 4% -> 2% of each run, Pallas kernels for 13% -> 31%
where the time goes in v2:
time: 289 us; the launch traced here: 288 us
  Pallas kernels  177 us (61%)
  waiting for transfers between devices  71.6 us (25%)
  starting transfers between devices  28.5 us (10%)
  local copies, waits for them, and re-layouts  5.77 us (2%)
  other arithmetic  3.51 us (1%)
    pallas_call x2, Pallas kernels, on_device(): pl.pallas_call(functools.partial(pack_kernel, first_slot=part * rcv_count...  114 us
    ppermute x21, waiting for transfers between devices, exchange(): lax.ppermute(array, axis, [(i, i ^ distance) for i in range(lax.axis_size...  45.7 us
    pallas_call x2, Pallas kernels, on_device(): pl.pallas_call(functools.partial(synthesis_kernel, receiver_tile=receiver...  38.7 us
    all_to_all x2, waiting for transfers between devices, on_device(): lax.all_to_all(sent[part], ('freq', 'rcv'), split_axis=0, concat_axis=0,...  25.9 us
    ppermute x21, starting transfers between devices, exchange(): lax.ppermute(array, axis, [(i, i ^ distance) for i in range(lax.axis_size...  22.1 us
    pallas_call x2, Pallas kernels, on_device(): sent.append(multiples(live, column, row, spectra, gains, *gathered[part]))  21.9 us
    all_to_all x2, starting transfers between devices, on_device(): lax.all_to_all(sent[part], ('freq', 'rcv'), split_axis=0, concat_axis=0,...  6.42 us
  transfers between devices with their start and end apart: 23, of which 11 were waited for; matrix products, arithmetic and copies ran while one was open for 2% of the time, Pallas kernels for 31%

profile of v2, /device:TPU:0, one launch (start us, length us, event | category | flops | bytes accessed | tf_op | source)
XLA Modules:
  0.0 287.6 jit_solution(1438223225196479620)
XLA Ops:
  0.0 56.8 %pack.2 = (f32[2,64,512]{2,1,0:T(8,128)}, f32[2,64,512]{2,1,0:T(8,128)}, f32[2,64,512]{2,1,0:T(8,128)}, f32[2,64,512]{2,1,0:T(8,128)}, f32[2,64,512]{2,1,0:T(8,1...) custom-call(f32[16,2,64,512]{3,2,1,0:T(8,128)} %spectra_ref.7), custom_call_target="tpu_custom_call" | custom-call | tf_op jit(solution)/shard_map/pack/pallas_call | solution.py:214
  57.3 3.7 %collective-permute-start.1 = (s32[64,128]{1,0:T(8,128)S(1)}, s32[64,128]{1,0:T(8,128)S(1)}, u32[]{:S(2)}, u32[]{:S(2)}) collective-permute-start(s32[64,128]{1,0:T(8,128)S(1)} %bitcast.37), channel_id=1, source_target_pairs={{0,16},{8,24},{16,0},{24,8},{1,17},{9,25},{17,1},{25,9},{2,18},{10... | collective-permute-start | bytes 98312 | tf_op jit(solution)/shard_map/ppermute | solution.py:192
  63.0 1.9 collective-permute-done
  64.9 3.4 %collective-permute-done.2 = s32[64,128]{1,0:T(8,128)S(1)} collective-permute-done((s32[64,128]{1,0:T(8,128)S(1)}, s32[64,128]{1,0:T(8,128)S(1)}, u32[]{:S(2)}, u32[]{:S(2)}) %collective-permute-start.2) | collective-permute-done | bytes 32800 | tf_op jit(solution)/shard_map/ppermute | solution.py:192
  68.3 2.5 collective-permute-start.6
  71.8 3.6 %collective-permute-done.6 = s32[4,64,128]{2,1,0:T(8,128)S(1)} collective-permute-done((s32[4,64,128]{2,1,0:T(8,128)S(1)}, s32[4,64,128]{2,1,0:T(8,128)S(1)}, u32[]{:S(2)}, u32[]{:S(2)}) %collective-permute-start.6) | collective-permute-done | bytes 131104 | tf_op jit(solution)/shard_map/ppermute | solution.py:192
  80.0 5.8 %collective-permute-done.15.refs_1_ = f32[2,64,512]{2,1,0:T(8,128)S(1)} collective-permute-done((f32[2,64,512]{2,1,0:T(8,128)}, f32[2,64,512]{2,1,0:T(8,128)S(1)}, u32[]{:S(2)}, u32[]{:S(2)}) %collective-permute-start.15) | collective-permute-done | bytes 262176 | tf_op jit(solution)/shard_map/ppermute | solution.py:192
  88.9 2.5 gains.1.gains_hbm
  92.8 10.5 %collective-permute-done.18.refs_4_ = f32[2,64,512]{2,1,0:T(8,128)S(1)} collective-permute-done((f32[2,64,512]{2,1,0:T(8,128)}, f32[2,64,512]{2,1,0:T(8,128)S(1)}, u32[]{:S(2)}, u32[]{:S(2)}) %collective-permute-start.18) | collective-permute-done | bytes 262176 | tf_op jit(solution)/shard_map/ppermute | solution.py:192
  103.3 10.9 %multiples.3 = f32[32,2,64,128]{3,2,1,0:T(8,128)S(1)} custom-call(s32[1]{0:T(128)} %bitcast.23.live_ref, s32[512,1]{1,0:T(8,128)S(1)} %copy.12.column_ref, s32[1,512]{1,0:T(1,128)S(1)} %bitcast.31, f32[16,2,64,512]{3,2,1,0:T(8,128)} %spectra_ref.7, f32[2,512,512]{2,1,0:T(8,128)} %copy-done, f32[2,64,512]{2,1,0:T(8,128)S(1)} %collective-permute-done.3.refs_0_, ...), custom_call_target="tpu_custom_call" | custom-call | tf_op jit(solution)/shard_map/multiples/pallas_call | solution.py:261
  115.6 2.7 all-to-all-start.1
  118.4 56.8 %pack.3 = (f32[2,64,512]{2,1,0:T(8,128)}, f32[2,64,512]{2,1,0:T(8,128)}, f32[2,64,512]{2,1,0:T(8,128)}, f32[2,64,512]{2,1,0:T(8,128)}, f32[2,64,512]{2,1,0:T(8,1...) custom-call(f32[16,2,64,512]{3,2,1,0:T(8,128)} %spectra_ref.7), custom_call_target="tpu_custom_call" | custom-call | tf_op jit(solution)/shard_map/pack/pallas_call | solution.py:214
  175.3 1.7 collective-permute-start.9
  177.1 1.7 collective-permute-start.11
  178.9 2.6 collective-permute-start.13
  181.4 3.2 %collective-permute-done.9.refs_1_ = f32[2,64,512]{2,1,0:T(8,128)S(1)} collective-permute-done((f32[2,64,512]{2,1,0:T(8,128)}, f32[2,64,512]{2,1,0:T(8,128)S(1)}, u32[]{:S(2)}, u32[]{:S(2)}) %collective-permute-start.9) | collective-permute-done | bytes 262176 | tf_op jit(solution)/shard_map/ppermute | solution.py:192
  186.5 3.1 %collective-permute-done.10.refs_2_ = f32[2,64,512]{2,1,0:T(8,128)S(1)} collective-permute-done((f32[2,64,512]{2,1,0:T(8,128)}, f32[2,64,512]{2,1,0:T(8,128)S(1)}, u32[]{:S(2)}, u32[]{:S(2)}) %collective-permute-start.10) | collective-permute-done | bytes 262176 | tf_op jit(solution)/shard_map/ppermute | solution.py:192
  189.6 12.8 %collective-permute-done.12.refs_4_ = f32[2,64,512]{2,1,0:T(8,128)} collective-permute-done((f32[2,64,512]{2,1,0:T(8,128)}, f32[2,64,512]{2,1,0:T(8,128)}, u32[]{:S(2)}, u32[]{:S(2)}) %collective-permute-start.12) | collective-permute-done | bytes 262176 | tf_op jit(solution)/shard_map/ppermute | solution.py:192
  202.4 10.9 %multiples.2 = f32[32,2,64,128]{3,2,1,0:T(8,128)S(1)} custom-call(s32[1]{0:T(128)} %bitcast.8.live_ref, s32[512,1]{1,0:T(8,128)S(1)} %copy.12.column_ref, s32[1,512]{1,0:T(1,128)S(1)} %bitcast.32, f32[16,2,64,512]{3,2,1,0:T(8,128)} %spectra_ref.7, f32[2,512,512]{2,1,0:T(8,128)} %copy-done, f32[2,64,512]{2,1,0:T(8,128)S(1)} %collective-permute-done.8.refs_0_, ...), custom_call_target="tpu_custom_call" | custom-call | tf_op jit(solution)/shard_map/multiples/pallas_call | solution.py:261
  214.7 3.7 %all-to-all-start = ((f32[32,2,64,128]{3,2,1,0:T(8,128)}), f32[32,2,64,128]{3,2,1,0:T(8,128)}, u32[]{:S(2)}, u32[]{:S(2)}) async-start(f32[32,2,64,128]{3,2,1,0:T(8,128)} %copy-done.2), calls=%async_computation | async-start | bytes 4194304 | tf_op jit(solution)/shard_map/all_to_all | solution.py:264
  219.2 2.5 add_add_fusion
  222.9 18.5 %synthesis.2.base_ref = f32[128,64,512]{2,1,0:T(8,128)} custom-call(f32[64,512]{1,0:T(8,128)S(1)} %reshape.309.table_ref, f32[4096,128]{1,0:T(8,128)S(1)} %bitcast.29, f32[128,64,512]{2,1,0:T(8,128)} %base_ref.1), custom_call_target="tpu_custom_call" | custom-call | tf_op jit(solution)/shard_map/synthesis/pallas_call | solution.py:274
  241.4 25.9 %all-to-all-done = f32[32,2,64,128]{3,2,1,0:T(8,128)} async-done(((f32[32,2,64,128]{3,2,1,0:T(8,128)}), f32[32,2,64,128]{3,2,1,0:T(8,128)}, u32[]{:S(2)}, u32[]{:S(2)}) %all-to-all-start) | async-done | bytes 2097184 | tf_op jit(solution)/shard_map/all_to_all | solution.py:264
  267.3 20.2 %synthesis.3 = f32[128,64,512]{2,1,0:T(8,128)} custom-call(f32[64,512]{1,0:T(8,128)S(1)} %reshape.305.table_ref, f32[4096,128]{1,0:T(8,128)} %bitcast.22.coef_hbm, f32[128,64,512]{2,1,0:T(8,128)} %synthesis.2.base_ref), custom_call_target="tpu_custom_call" | custom-call | tf_op jit(solution)/shard_map/synthesis/pallas_call | solution.py:274
  (61 shorter events, 18.1 us)
Async XLA Ops:
  0.0 88.9 %copy-start.4 = (f32[2,16]{1,0:T(2,128)S(1)}, f32[2,16]{1,0:T(2,128)}, u32[]{:S(2)}) copy-start(f32[2,16]{1,0:T(2,128)} %table_ref.1) | copy-start | bytes 388
  56.8 11.5 %collective-permute-start.3 = (f32[2,64,512]{2,1,0:T(8,128)}, f32[2,64,512]{2,1,0:T(8,128)S(1)}, u32[]{:S(2)}, u32[]{:S(2)}) collective-permute-start(f32[2,64,512]{2,1,0:T(8,128)} %get-tuple-element.22), channel_id=1, source_target_pairs={{0,1},{1,0},{2,3},{3,2},{4,5},{5,4},{6,7},{7,6},{8,9},{9,8},{10,11... | collective-permute-start | bytes 786440 | tf_op jit(solution)/shard_map/ppermute | solution.py:192
  57.3 5.6 %collective-permute-start.1 = (s32[64,128]{1,0:T(8,128)S(1)}, s32[64,128]{1,0:T(8,128)S(1)}, u32[]{:S(2)}, u32[]{:S(2)}) collective-permute-start(s32[64,128]{1,0:T(8,128)S(1)} %bitcast.37), channel_id=1, source_target_pairs={{0,16},{8,24},{16,0},{24,8},{1,17},{9,25},{17,1},{25,9},{2,18},{10... | collective-permute-start | bytes 98312 | tf_op jit(solution)/shard_map/ppermute | solution.py:192
  61.0 3.9 %collective-permute-start = (s32[64,128]{1,0:T(8,128)S(1)}, s32[64,128]{1,0:T(8,128)S(1)}, u32[]{:S(2)}, u32[]{:S(2)}) collective-permute-start(s32[64,128]{1,0:T(8,128)S(1)} %bitcast.38), channel_id=1, source_target_pairs={{0,8},{8,0},{16,24},{24,16},{1,9},{9,1},{17,25},{25,17},{2,10},{10... | collective-permute-start | bytes 98312 | tf_op jit(solution)/shard_map/ppermute | solution.py:192
  62.6 5.7 %collective-permute-start.2 = (s32[64,128]{1,0:T(8,128)S(1)}, s32[64,128]{1,0:T(8,128)S(1)}, u32[]{:S(2)}, u32[]{:S(2)}) collective-permute-start(s32[64,128]{1,0:T(8,128)S(1)} %bitcast.39), channel_id=1, source_target_pairs={{0,24},{8,16},{16,8},{24,0},{1,25},{9,17},{17,9},{25,1},{2,26},{10... | collective-permute-start | bytes 98312 | tf_op jit(solution)/shard_map/ppermute | solution.py:192
  68.3 7.1 %collective-permute-start.6 = (s32[4,64,128]{2,1,0:T(8,128)S(1)}, s32[4,64,128]{2,1,0:T(8,128)S(1)}, u32[]{:S(2)}, u32[]{:S(2)}) collective-permute-start(s32[4,64,128]{2,1,0:T(8,128)S(1)} %pad_add_fusion.1), channel_id=1, source_target_pairs={{0,6},{1,7},{2,4},{3,5},{4,2},{5,3},{6,0},{7,1},{8,14},{9,15},{10,... | collective-permute-start | bytes 393224 | tf_op jit(solution)/shard_map/ppermute | solution.py:192
  70.8 5.5 %collective-permute-start.5 = (s32[4,64,128]{2,1,0:T(8,128)S(1)}, s32[4,64,128]{2,1,0:T(8,128)S(1)}, u32[]{:S(2)}, u32[]{:S(2)}) collective-permute-start(s32[4,64,128]{2,1,0:T(8,128)S(1)} %pad_add_fusion.1), channel_id=1, source_target_pairs={{0,4},{1,5},{2,6},{3,7},{4,0},{5,1},{6,2},{7,3},{8,12},{9,13},{10,... | collective-permute-start | bytes 393224 | tf_op jit(solution)/shard_map/ppermute | solution.py:192
  71.3 5.0 %collective-permute-start.4 = (s32[4,64,128]{2,1,0:T(8,128)S(1)}, s32[4,64,128]{2,1,0:T(8,128)S(1)}, u32[]{:S(2)}, u32[]{:S(2)}) collective-permute-start(s32[4,64,128]{2,1,0:T(8,128)S(1)} %pad_add_fusion.1), channel_id=1, source_target_pairs={{0,2},{1,3},{2,0},{3,1},{4,6},{5,7},{6,4},{7,5},{8,10},{9,11},{10,... | collective-permute-start | bytes 393224 | tf_op jit(solution)/shard_map/ppermute | solution.py:192
  76.4 11.1 %collective-permute-start.7 = (s32[4,4,64,128]{3,2,1,0:T(8,128)S(1)}, s32[4,4,64,128]{3,2,1,0:T(8,128)S(1)}, u32[]{:S(2)}, u32[]{:S(2)}) collective-permute-start(s32[4,4,64,128]{3,2,1,0:T(8,128)S(1)} %pad_add_fusion.near_ref), channel_id=1, source_target_pairs={{0,1},{1,0},{2,3},{3,2},{4,5},{5,4},{6,7},{7,6},{8,9},{9,8},{10,11... | collective-permute-start | bytes 1572872 | tf_op jit(solution)/shard_map/ppermute | solution.py:192
  76.4 9.4 %collective-permute-start.15 = (f32[2,64,512]{2,1,0:T(8,128)}, f32[2,64,512]{2,1,0:T(8,128)S(1)}, u32[]{:S(2)}, u32[]{:S(2)}) collective-permute-start(f32[2,64,512]{2,1,0:T(8,128)} %get-tuple-element.32), channel_id=1, source_target_pairs={{0,2},{1,3},{2,0},{3,1},{4,6},{5,7},{6,4},{7,5},{8,10},{9,11},{10,... | collective-permute-start | bytes 786440 | tf_op jit(solution)/shard_map/ppermute | solution.py:192
  78.0 14.8 %collective-permute-start.16 = (f32[2,64,512]{2,1,0:T(8,128)}, f32[2,64,512]{2,1,0:T(8,128)S(1)}, u32[]{:S(2)}, u32[]{:S(2)}) collective-permute-start(f32[2,64,512]{2,1,0:T(8,128)} %get-tuple-element.33), channel_id=1, source_target_pairs={{0,3},{1,2},{2,1},{3,0},{4,7},{5,6},{6,5},{7,4},{8,11},{9,10},{10,... | collective-permute-start | bytes 786440 | tf_op jit(solution)/shard_map/ppermute | solution.py:192
  78.3 14.5 %collective-permute-start.17 = (f32[2,64,512]{2,1,0:T(8,128)}, f32[2,64,512]{2,1,0:T(8,128)S(1)}, u32[]{:S(2)}, u32[]{:S(2)}) collective-permute-start(f32[2,64,512]{2,1,0:T(8,128)} %get-tuple-element.34), channel_id=1, source_target_pairs={{0,4},{1,5},{2,6},{3,7},{4,0},{5,1},{6,2},{7,3},{8,12},{9,13},{10,... | collective-permute-start | bytes 786440 | tf_op jit(solution)/shard_map/ppermute | solution.py:192
  79.8 23.6 %collective-permute-start.18 = (f32[2,64,512]{2,1,0:T(8,128)}, f32[2,64,512]{2,1,0:T(8,128)S(1)}, u32[]{:S(2)}, u32[]{:S(2)}) collective-permute-start(f32[2,64,512]{2,1,0:T(8,128)} %get-tuple-element.35), channel_id=1, source_target_pairs={{0,5},{1,4},{2,7},{3,6},{4,1},{5,0},{6,3},{7,2},{8,13},{9,12},{10,... | collective-permute-start | bytes 786440 | tf_op jit(solution)/shard_map/ppermute | solution.py:192
  85.8 17.5 %collective-permute-start.19 = (f32[2,64,512]{2,1,0:T(8,128)}, f32[2,64,512]{2,1,0:T(8,128)S(1)}, u32[]{:S(2)}, u32[]{:S(2)}) collective-permute-start(f32[2,64,512]{2,1,0:T(8,128)} %get-tuple-element.36), channel_id=1, source_target_pairs={{0,6},{1,7},{2,4},{3,5},{4,2},{5,3},{6,0},{7,1},{8,14},{9,15},{10,... | collective-permute-start | bytes 786440 | tf_op jit(solution)/shard_map/ppermute | solution.py:192
  87.5 15.9 %collective-permute-start.20 = (f32[2,64,512]{2,1,0:T(8,128)}, f32[2,64,512]{2,1,0:T(8,128)S(1)}, u32[]{:S(2)}, u32[]{:S(2)}) collective-permute-start(f32[2,64,512]{2,1,0:T(8,128)} %get-tuple-element.37), channel_id=1, source_target_pairs={{0,7},{1,6},{2,5},{3,4},{4,3},{5,2},{6,1},{7,0},{8,15},{9,14},{10,... | collective-permute-start | bytes 786440 | tf_op jit(solution)/shard_map/ppermute | solution.py:192
  115.6 99.0 %all-to-all-start.1 = ((f32[32,2,64,128]{3,2,1,0:T(8,128)}), f32[32,2,64,128]{3,2,1,0:T(8,128)S(1)}, u32[]{:S(2)}, u32[]{:S(2)}) async-start(f32[32,2,64,128]{3,2,1,0:T(8,128)} %copy-done.1), calls=%async_computation.1 | async-start | bytes 4194304 | tf_op jit(solution)/shard_map/all_to_all | solution.py:264
  175.1 3.7 %collective-permute-start.8 = (f32[2,64,512]{2,1,0:T(8,128)}, f32[2,64,512]{2,1,0:T(8,128)S(1)}, u32[]{:S(2)}, u32[]{:S(2)}) collective-permute-start(f32[2,64,512]{2,1,0:T(8,128)} %get-tuple-element.24), channel_id=1, source_target_pairs={{0,1},{1,0},{2,3},{3,2},{4,5},{5,4},{6,7},{7,6},{8,9},{9,8},{10,11... | collective-permute-start | bytes 786440 | tf_op jit(solution)/shard_map/ppermute | solution.py:192
  175.3 9.3 %collective-permute-start.9 = (f32[2,64,512]{2,1,0:T(8,128)}, f32[2,64,512]{2,1,0:T(8,128)S(1)}, u32[]{:S(2)}, u32[]{:S(2)}) collective-permute-start(f32[2,64,512]{2,1,0:T(8,128)} %get-tuple-element.25), channel_id=1, source_target_pairs={{0,2},{1,3},{2,0},{3,1},{4,6},{5,7},{6,4},{7,5},{8,10},{9,11},{10,... | collective-permute-start | bytes 786440 | tf_op jit(solution)/shard_map/ppermute | solution.py:192
  177.0 12.6 %collective-permute-start.10 = (f32[2,64,512]{2,1,0:T(8,128)}, f32[2,64,512]{2,1,0:T(8,128)S(1)}, u32[]{:S(2)}, u32[]{:S(2)}) collective-permute-start(f32[2,64,512]{2,1,0:T(8,128)} %get-tuple-element.26), channel_id=1, source_target_pairs={{0,3},{1,2},{2,1},{3,0},{4,7},{5,6},{6,5},{7,4},{8,11},{9,10},{10,... | collective-permute-start | bytes 786440 | tf_op jit(solution)/shard_map/ppermute | solution.py:192
  177.1 12.5 %collective-permute-start.11 = (f32[2,64,512]{2,1,0:T(8,128)}, f32[2,64,512]{2,1,0:T(8,128)S(1)}, u32[]{:S(2)}, u32[]{:S(2)}) collective-permute-start(f32[2,64,512]{2,1,0:T(8,128)} %get-tuple-element.27), channel_id=1, source_target_pairs={{0,4},{1,5},{2,6},{3,7},{4,0},{5,1},{6,2},{7,3},{8,12},{9,13},{10,... | collective-permute-start | bytes 786440 | tf_op jit(solution)/shard_map/ppermute | solution.py:192
  178.7 23.7 %collective-permute-start.12 = (f32[2,64,512]{2,1,0:T(8,128)}, f32[2,64,512]{2,1,0:T(8,128)}, u32[]{:S(2)}, u32[]{:S(2)}) collective-permute-start(f32[2,64,512]{2,1,0:T(8,128)} %get-tuple-element.28), channel_id=1, source_target_pairs={{0,5},{1,4},{2,7},{3,6},{4,1},{5,0},{6,3},{7,2},{8,13},{9,12},{10,... | collective-permute-start | bytes 786440 | tf_op jit(solution)/shard_map/ppermute | solution.py:192
  178.9 23.6 %collective-permute-start.13 = (f32[2,64,512]{2,1,0:T(8,128)}, f32[2,64,512]{2,1,0:T(8,128)}, u32[]{:S(2)}, u32[]{:S(2)}) collective-permute-start(f32[2,64,512]{2,1,0:T(8,128)} %get-tuple-element.29), channel_id=1, source_target_pairs={{0,6},{1,7},{2,4},{3,5},{4,2},{5,3},{6,0},{7,1},{8,14},{9,15},{10,... | collective-permute-start | bytes 786440 | tf_op jit(solution)/shard_map/ppermute | solution.py:192
  184.7 17.7 %collective-permute-start.14 = (f32[2,64,512]{2,1,0:T(8,128)}, f32[2,64,512]{2,1,0:T(8,128)}, u32[]{:S(2)}, u32[]{:S(2)}) collective-permute-start(f32[2,64,512]{2,1,0:T(8,128)} %get-tuple-element.30), channel_id=1, source_target_pairs={{0,7},{1,6},{2,5},{3,4},{4,3},{5,2},{6,1},{7,0},{8,15},{9,14},{10,... | collective-permute-start | bytes 786440 | tf_op jit(solution)/shard_map/ppermute | solution.py:192
  214.7 52.6 %all-to-all-start = ((f32[32,2,64,128]{3,2,1,0:T(8,128)}), f32[32,2,64,128]{3,2,1,0:T(8,128)}, u32[]{:S(2)}, u32[]{:S(2)}) async-start(f32[32,2,64,128]{3,2,1,0:T(8,128)} %copy-done.2), calls=%async_computation | async-start | bytes 4194304 | tf_op jit(solution)/shard_map/all_to_all | solution.py:264
  (6 other events, 237.5 us)
